TPU v7x, 32 devices: a whole 2x2x4 slice. The times are simulated.
32 devices in a mesh: row: 4 (over y, x), col: 8 (over z, core).
Axes of the slice: x: 2, y: 2, z: 4, core: 2. Of those that a mesh axis runs over, the one named last changes fastest.
Arguments:
- three_center: bfloat16 [4096, 6144], P(('row', 'col')), may hold values from -6 to 6
- density: bfloat16 [4096, 4096], P('row', 'col'), may hold values from -0.1875 to 0.1875
- block_mask: int32 [128, 48], P(('row', 'col')), may hold values 0 or 1
- density_mask: int32 [128, 128], P('row', 'col'), may hold values 0 or 1
- basis_count: int32 [128], replicated, may hold values from 8 to 32
- ri_count: int32 [48], replicated, may hold values from 16 to 128
Outputs:
- contracted: bfloat16 [4096, 6144], P('row', 'col')
All inputs are finite; a program needn't handle non-finite values. No bound on the sum of `block_mask` or of `density_mask` on one device may be relied on, other than what follows from the above.
Results may differ from a plain program's by a relative error of at most 0.001.
Values may be sent and summed in bfloat16 or wider, within the bound.
No kernel may reach another device: no remote copies, remote signals or barrier semaphores. Data moves between devices by JAX's collectives and lax.ppermute only.
A program may use at most 64 MiB of HBM per device.

v0:
```python
import jax
import jax.numpy as jnp
from jax import lax
from jax.experimental import pallas as pl
from jax.experimental.pallas import tpu as pltpu
from jax.sharding import PartitionSpec as P

BW = 32
RW = 128
CORES = 2
VMEM = 48 * 1024 * 1024
BF16 = jnp.bfloat16
F32 = jnp.float32
SMEM_SPEC = pl.BlockSpec(memory_space=pltpu.SMEM)
VMEM_SPEC = pl.BlockSpec(memory_space=pltpu.VMEM)
ANY_SPEC = pl.BlockSpec(memory_space=pl.ANY)


def params(limit=VMEM):
    return pltpu.CompilerParams(vmem_limit_bytes=limit)


def cost(flops, bytes_accessed):
    return pl.CostEstimate(flops=flops, bytes_accessed=bytes_accessed, transcendentals=0)


def ones_where(cond):
    return jnp.where(cond, 1.0, 0.0).astype(BF16)


def iota(shape, axis):
    return lax.broadcasted_iota(jnp.int32, shape, axis)


def loop(n, unroll):
    def run(f):
        if unroll:
            for i in range(n):
                f(i)
        else:
            pl.loop(0, n)(f)

    return run


def span(i, size):
    return pl.ds(i * size if isinstance(i, int) else pl.multiple_of(i * size, size), size)


def place_row(count_ref, base, atoms, width):
    lane = iota((1, atoms * width), 1)

    def atom(a, carry):
        place, offset = carry
        count = count_ref[base + a]
        inside = (lane >= a * width) & (lane < a * width + count)
        return jnp.where(inside, lane - a * width + offset, place), offset + count

    return lax.fori_loop(0, atoms, atom, (jnp.full(lane.shape, -1, jnp.int32), jnp.int32(0)))[0]


def pack_rows(count_ref, base, atoms, width, size):
    place = place_row(count_ref, base, atoms, width)
    return ones_where(iota((size, atoms * width), 0) == place)


def pack_cols(count_ref, base, atoms, width, size, out, unroll):
    def atom(a, offset):
        count = count_ref[base + a]
        slot = iota((width, size), 0)
        gap = iota((width, size), 1) - slot
        out[span(a, width), :] = ones_where((gap == offset) & (slot < count))
        return offset + count

    if unroll:
        offset = jnp.int32(0)
        for a in range(atoms):
            offset = atom(a, offset)
    else:
        lax.fori_loop(0, atoms, atom, jnp.int32(0))


def first_fit(count_ref, ri_ref, groups, levels):
    level = jnp.int32(0)
    for axis, (ref, parts) in enumerate(zip((count_ref, count_ref, ri_ref), groups)):
        per = ref.shape[0] // parts
        most = jnp.int32(0)
        for g in range(parts):
            total = jnp.int32(0)
            for i in range(per):
                total = total + ref[g * per + i]
            most = jnp.maximum(most, total)
        for n, sizes in enumerate(levels[:-1]):
            level = jnp.where(most > sizes[axis], jnp.maximum(level, n + 1), level)
    return level


def pack_integrals(tc, block_mask, basis_count, ri_count, ncols, packed, unroll, arrived=None, levels=None):
    rows, cols = tc.shape
    atoms = rows // BW
    wide = cols // ncols
    blocks = wide // RW
    chips = ncols // CORES
    first = arrived is None

    def body(count_ref, ri_ref, mask_ref, x_ref, *refs):
        if levels is not None:
            refs[1][0] = first_fit(count_ref, ri_ref, *levels)
        outs = refs[:1] if first else refs[1 : 1 + chips]
        held, hot = refs[-2:] if first else refs[-3:-1]
        made = outs[0] if first else refs[-1]
        row, col = lax.axis_index("row"), lax.axis_index("col")
        base = (row * ncols + col) * atoms

        @loop(chips, unroll)
        def _(t):
            dest = col ^ (CORES * t + (1 if first else 0))

            @loop(blocks, unroll)
            def _(b):
                lanes = pl.ds(pl.multiple_of(dest * wide + b * RW, RW), RW)
                slot = iota((BW, RW), 0)
                for a in range(atoms):
                    limit = jnp.where(mask_ref[a, dest * blocks + b] > 0, count_ref[base + a], 0)
                    x = x_ref[pl.ds(a * BW, BW), lanes].astype(F32)
                    held[pl.ds(a * BW, BW), span(b, RW)] = jnp.where(slot < limit, x, 0.0).astype(BF16)

            pack_cols(ri_ref, dest * blocks, blocks, RW, packed, hot, unroll)
            made[t] = jnp.dot(held[...], hot[...], preferred_element_type=F32).astype(BF16)

        if not first:
            core = lax.rem(col, CORES)
            for t in range(chips):
                outs[t][pl.ds(pl.multiple_of(core * rows, rows), rows), :] = made[t]
                outs[t][pl.ds(pl.multiple_of((1 - core) * rows, rows), rows), :] = refs[0][t]

    shape = (chips, rows, packed)
    merged = jax.ShapeDtypeStruct((CORES * rows, packed), BF16)
    out_shape = [jax.ShapeDtypeStruct(shape, BF16)] if first else [merged] * chips
    out_specs = [VMEM_SPEC] * len(out_shape)
    if levels is not None:
        out_shape.append(jax.ShapeDtypeStruct((1,), jnp.int32))
        out_specs.append(SMEM_SPEC)
    return pl.pallas_call(
        body,
        out_shape=out_shape,
        in_specs=[SMEM_SPEC, SMEM_SPEC, SMEM_SPEC] + [VMEM_SPEC] * (1 if first else 2),
        out_specs=out_specs,
        scratch_shapes=[pltpu.VMEM((rows, wide), BF16), pltpu.VMEM((wide, packed), BF16)]
        + ([] if first else [pltpu.VMEM(shape, BF16)]),
        compiler_params=params(),
        cost_estimate=cost(rows * cols * packed, rows * cols + 3 * chips * rows * packed),
        name="pack_other_core" if first else "pack_own_core",
    )(basis_count, ri_count, block_mask, tc, *([] if first else [arrived]))


def pack_density(dens, mask, basis_count, lam_size, sum_size, unroll):
    rows, cols = dens.shape
    lam_atoms, sum_atoms = mask.shape
    steps = 1 if unroll else 4
    tile = rows // steps
    out_tile = lam_size // steps

    def body(count_ref, mask_ref, x_ref, o_ref, hot, keep, mid):
        row, col = lax.axis_index("row"), lax.axis_index("col")
        of_atom = ones_where(iota((sum_atoms, cols), 1) // BW == iota((sum_atoms, cols), 0))
        keep[...] = jnp.dot(ones_where(mask_ref[...] > 0), of_atom, preferred_element_type=F32).astype(BF16)
        pack_cols(count_ref, col * sum_atoms, sum_atoms, BW, sum_size, hot, unroll)

        @loop(steps, unroll)
        def _(i):
            at = span(i, tile)
            shape = (tile, lam_atoms)
            atom = ones_where((iota(shape, 0) + i * tile) // BW == iota(shape, 1))
            kept = jnp.dot(atom, keep[...], preferred_element_type=F32)
            x = jnp.where(kept > 0.5, x_ref[at, :].astype(F32), 0.0).astype(BF16)
            mid[at, :] = jnp.dot(x, hot[...], preferred_element_type=F32).astype(BF16)

        place = place_row(count_ref, row * lam_atoms, lam_atoms, BW)

        @loop(steps, unroll)
        def _(i):
            at = span(i, out_tile)
            left = ones_where(iota((out_tile, rows), 0) + i * out_tile == place)
            o_ref[at, :] = jnp.dot(left, mid[...], preferred_element_type=F32).astype(BF16)

    return pl.pallas_call(
        body,
        out_shape=jax.ShapeDtypeStruct((lam_size, sum_size), BF16),
        in_specs=[SMEM_SPEC, VMEM_SPEC, VMEM_SPEC],
        out_specs=VMEM_SPEC,
        scratch_shapes=[
            pltpu.VMEM((cols, sum_size), BF16),
            pltpu.VMEM((lam_atoms, cols), BF16),
            pltpu.VMEM((rows, sum_size), BF16),
        ],
        compiler_params=params(),
        cost_estimate=cost(2 * rows * sum_size * (cols + lam_size), 2 * rows * cols),
        name="pack_density",
    )(basis_count, mask, dens)


def pack_part(pieces, basis_count, first, ncols, size):
    rows, cols = pieces[0].shape
    per = len(pieces)
    depth = per * rows
    atoms = depth // BW

    def body(count_ref, *refs):
        blocks, o_ref, full = refs[:per], refs[per], refs[per + 1]
        row, chip = lax.axis_index("row"), lax.axis_index("col") // CORES
        for i in range(per):
            at = lax.rem(chip ^ (first + i), per) * rows
            full[pl.ds(pl.multiple_of(at, rows), rows), :] = blocks[i][...]
        part = (row * (ncols // CORES) + (chip ^ first)) * rows // depth
        hot = pack_rows(count_ref, part * atoms, atoms, BW, size)
        o_ref[...] = jnp.dot(hot, full[...], preferred_element_type=F32).astype(BF16)

    return pl.pallas_call(
        body,
        out_shape=jax.ShapeDtypeStruct((size, cols), BF16),
        in_specs=[SMEM_SPEC] + [VMEM_SPEC] * per,
        out_specs=VMEM_SPEC,
        scratch_shapes=[pltpu.VMEM((depth, cols), BF16)],
        compiler_params=params(),
        cost_estimate=cost((2 + 10 * first) * size * depth * cols, 2 * cols * (depth + size)),
        name="pack_part",
    )(basis_count, *pieces)


def exchange(x, axis, bit):
    peers = lax.axis_size(axis)
    return lax.ppermute(x, axis, [(i, i ^ bit) for i in range(peers)])


def after(x, *others):
    return lax.optimization_barrier((x, *others))[0]


def double(own, axis, bits):
    have = {0: own}
    for bit in bits:
        for far in sorted(have):
            have[far | bit] = exchange(have[far], axis, bit)
    return have


def add_parts(total, tile, unroll, d_refs, sums, before=None):
    lam, cols = total.shape

    @loop(lam // tile, unroll)
    def _(j):
        out = span(j, tile)
        x = None if before is None else before[out, :]
        for chunks, part in zip(d_refs, sums):
            if len(chunks) == 1:
                d = chunks[0][out, :]
            elif isinstance(j, int):
                size = chunks[0].shape[0]
                d = chunks[j * tile // size][pl.ds(j * tile % size, tile), :]
            else:
                per = chunks[0].shape[0] // tile
                inner = span(lax.rem(j, per), tile)
                d = jnp.where(j < per, chunks[0][inner, :].astype(F32), chunks[1][inner, :].astype(F32)).astype(BF16)
            y = jnp.dot(d, part(), preferred_element_type=F32)
            x = y if x is None else x + y
        total[out, :] = x


def split_refs(dens, refs):
    lists, at = [], 0
    for chunks in dens.values():
        lists.append(refs[at : at + len(chunks)])
        at += len(chunks)
    return lists, refs[at:]


def flat(dens):
    return [chunk for chunks in dens.values() for chunk in chunks]


def contract_near(dens, integrals, basis_count, ri_count, ncols, rows, wide, unroll):
    lam, depth = dens[0][0].shape
    groups, nrows = len(integrals), len(integrals[0])
    sums = [integrals[g][far] for far in range(nrows) for g in range(groups)]
    cols = sums[0].shape[1]
    lam_atoms, blocks = rows // BW, wide // RW
    n, parts = len(dens), len(sums)

    def body(count_ref, ri_ref, *refs):
        d_refs, refs = split_refs(dens, refs)
        s_refs, refs = refs[:parts], refs[parts:]
        total, lam_hot, col_hot, s_rest, s_all, s_sem, r_sem = refs
        row, col = lax.axis_index("row"), lax.axis_index("col")
        for j, ref in enumerate(s_refs):
            part = (row ^ (j // groups)) * groups + (col // (ncols // groups) ^ (j % groups))
            pltpu.make_async_copy(ref, s_all.at[part], s_sem.at[part]).start()
        pack_cols(count_ref, row * lam_atoms, lam_atoms, BW, lam, lam_hot, unroll)
        place = place_row(ri_ref, col * blocks, blocks, RW)

        @loop(cols // RW, unroll)
        def _(i):
            col_hot[span(i, RW), :] = ones_where(iota((RW, wide), 0) + i * RW == place)

        @pl.loop(0, parts)
        def _(i):
            pltpu.make_async_copy(s_all.at[i], s_all.at[i], s_sem.at[i]).wait()

        rest = [pltpu.make_async_copy(s_all.at[col ^ far], s_rest.at[far - n], r_sem.at[far - n]) for far in range(n, parts)]
        for copy in rest:
            copy.start()
        add_parts(total, lam // 2, unroll, d_refs, [lambda far=far: s_all[col ^ far] for far in range(n)])
        for copy in rest:
            copy.wait()

    need = 2 * (n * depth * lam + 2 * parts * depth * cols + 4 * lam * cols + rows * lam + cols * wide)
    return pl.pallas_call(
        body,
        out_shape=[
            jax.ShapeDtypeStruct((lam, cols), F32),
            jax.ShapeDtypeStruct((rows, lam), BF16),
            jax.ShapeDtypeStruct((cols, wide), BF16),
            jax.ShapeDtypeStruct((parts - n, depth, cols), BF16),
        ],
        in_specs=[SMEM_SPEC, SMEM_SPEC] + [VMEM_SPEC] * n + [ANY_SPEC] * parts,
        out_specs=[VMEM_SPEC] * 4,
        scratch_shapes=[
            pltpu.VMEM((parts, depth, cols), BF16),
            pltpu.SemaphoreType.DMA((parts,)),
            pltpu.SemaphoreType.DMA((parts - n,)),
        ],
        compiler_params=params(need + 4 * 1024 * 1024),
        cost_estimate=cost(2 * n * depth * lam * cols, 2 * n * depth * (lam + cols)),
        name="contract_near",
    )(basis_count, ri_count, *flat(dens), *sums)


def contract_far(dens, first, total, sums, unroll):
    (lam, cols), depth = total.shape, sums.shape[1]
    n = len(dens)

    def body(before, s_ref, *refs):
        d_refs, (o_ref,) = split_refs(dens, refs)
        add_parts(o_ref, lam // 2, unroll, d_refs, [lambda i=i: s_ref[first + i] for i in range(n)], before)

    need = 2 * (n * depth * lam + sums.size + 4 * lam * cols)
    return pl.pallas_call(
        body,
        out_shape=jax.ShapeDtypeStruct((lam, cols), F32),
        in_specs=[VMEM_SPEC] * (2 + len(flat(dens))),
        out_specs=VMEM_SPEC,
        compiler_params=params(need + 4 * 1024 * 1024),
        cost_estimate=cost(2 * n * depth * lam * cols, 2 * n * depth * (lam + cols)),
        name="contract_far",
    )(total, sums, *flat(dens))


def contract_last(dens, first, total, sums, lam_hot, col_hot, unroll):
    (rows, lam), (cols, wide) = lam_hot.shape, col_hot.shape
    depth = sums.shape[1]
    n = len(dens)
    half = lam // 2

    def body(before, s_ref, lam_hot, col_hot, *refs):
        d_refs, (o_ref, total, packed, made, sem) = split_refs(dens, refs)
        add_parts(total, half, unroll, d_refs, [lambda i=i: s_ref[first + i] for i in range(n)], before)

        @loop(2, unroll)
        def _(j):
            x = total[span(j, half), :].astype(BF16)
            packed[span(j, half), :] = jnp.dot(x, col_hot[...], preferred_element_type=F32).astype(BF16)

        copies = []
        for j in range(4):
            out = span(j, rows // 4)
            made[out, :] = jnp.dot(lam_hot[out, :], packed[...], preferred_element_type=F32).astype(BF16)
            copies.append(pltpu.make_async_copy(made.at[out, :], o_ref.at[out, :], sem.at[j]))
            copies[-1].start()
        for copy in copies:
            copy.wait()

    need = 2 * (n * depth * lam + sums.size + 4 * lam * cols + rows * lam + cols * wide + (lam + rows) * wide)
    return pl.pallas_call(
        body,
        out_shape=jax.ShapeDtypeStruct((rows, wide), BF16),
        in_specs=[VMEM_SPEC] * (4 + len(flat(dens))),
        out_specs=ANY_SPEC,
        scratch_shapes=[
            pltpu.VMEM((lam, cols), F32),
            pltpu.VMEM((lam, wide), BF16),
            pltpu.VMEM((rows, wide), BF16),
            pltpu.SemaphoreType.DMA((4,)),
        ],
        compiler_params=params(need + 4 * 1024 * 1024),
        cost_estimate=cost(2 * n * depth * lam * cols, 2 * n * depth * (lam + cols)),
        name="contract_last",
    )(total, sums, lam_hot, col_hot, *flat(dens))


def program(lam_size, sum_size, col_size, common):
    unroll = common

    def run(three_center, density, block_mask, density_mask, basis_count, ri_count, other):
        ncols = lax.axis_size("col")
        nrows = lax.axis_size("row")
        chips = ncols // CORES
        rows, depth = density.shape
        wide = three_center.shape[1] // ncols
        row_bits = [1 << b for b in range(nrows.bit_length() - 1)]
        chip_bits = [CORES << b for b in range(chips.bit_length() - 1)][::-1]
        far_bit, near_bits = chip_bits[0], chip_bits[1:]

        counts = (block_mask, basis_count, ri_count, ncols, col_size, unroll)
        if not common:
            other = pack_integrals(three_center, *counts)[0]
        other = exchange(other, "col", 1)
        own = pack_density(density, density_mask, basis_count, lam_size, sum_size, unroll)
        near = {0: own, 1: exchange(own, "col", 1)}
        pieces = pack_integrals(three_center, *counts, after(other, own))
        got = [pieces[0]] + [exchange(pieces[t], "col", CORES * t) for t in range(1, chips)]
        per = depth // pieces[0].shape[0]
        parts, groups, orders = [], [], []
        for g in range(chips // per):
            arrived = got[g * per : (g + 1) * per]
            if g == 0:
                arrived = [after(arrived[0], near[1])] + arrived[1:]
            part = pack_part(arrived, basis_count, g * per, ncols, sum_size)
            if g == 0:
                near.update(double(after(own, part), "col", near_bits))
                steps = [near[far] for far in near if far > 1]
            else:
                part = after(part, *[groups[0][bit] for bit in row_bits])
            parts.append(part)
            orders.append(row_bits if g % 2 == 0 else row_bits[::-1])
            groups.append({0: part})
            for i, bit in enumerate(orders[g]):
                groups[g][bit] = exchange(after(part, *steps) if g > 0 and i > 0 else part, "row", bit)
        step = groups[-1][orders[-1][0]]
        line = {0: own, far_bit: exchange(after(own, parts[-1]), "col", far_bit)}
        for g, have in enumerate(groups):
            done = [0, orders[g][0]]
            for bit in orders[g][1:]:
                for far in done[1:]:
                    have[far | bit] = exchange(have[far] if g == len(groups) - 1 else after(have[far], step), "row", bit)
                done += [far | bit for far in done]
        for far in [far for far in near if far > 1]:
            near[far | 1] = exchange(near[far], "col", 1)
        first = {far: [near[far]] for far in sorted(near)}
        total, lam_hot, col_hot, sums = contract_near(
            first, groups, basis_count, ri_count, ncols, rows, wide, unroll
        )
        for away, block in double(line[far_bit], "col", near_bits).items():
            line[far_bit | away] = block
        middle = {}
        for far in range(far_bit, ncols - CORES, CORES):
            middle[far] = [line[far]]
            middle[far | 1] = [exchange(line[far], "col", 1)]
        total = contract_far(middle, 0, total, sums, unroll)
        end = line[ncols - CORES]
        last = {ncols - CORES: [end], ncols - 1: [exchange(after(end, total), "col", 1)]}
        return contract_last(last, len(middle), total, sums, lam_hot, col_hot, unroll)

    return run


def choose(here, yes, no):
    return lambda *args: lax.cond(here, yes, no, *args)


def shards(three_center, density, block_mask, density_mask, basis_count, ri_count):
    ncols = lax.axis_size("col")
    nrows = lax.axis_size("row")
    rows, depth = density.shape
    wide = three_center.shape[1] // ncols
    levels = (
        (rows * 3 // 4, depth * 3 // 4, wide * 5 // 6),
        (rows * 3 // 4, depth, wide * 5 // 6),
        (rows * 3 // 4, depth, wide),
        (rows, depth, wide),
    )
    other, level = pack_integrals(
        three_center,
        block_mask,
        basis_count,
        ri_count,
        ncols,
        levels[0][2],
        True,
        levels=((nrows, ncols, ncols), levels),
    )
    args = (three_center, density, block_mask, density_mask, basis_count, ri_count, other)
    run = program(*levels[-1], False)
    for n in reversed(range(len(levels) - 1)):
        run = choose(level[0] == n, program(*levels[n], n == 0), run)
    return run(*args)


def solution(mesh):
    in_specs = (
        P(("row", "col"), None),
        P("row", "col"),
        P(("row", "col"), None),
        P("row", "col"),
        P(),
        P(),
    )
    return jax.shard_map(
        shards, mesh=mesh, in_specs=in_specs, out_specs=P("row", "col"), check_vma=False
    )
```

profile of v0, /device:TPU:0, one launch (start us, length us, event | category | flops | bytes accessed | tf_op | source)
XLA Modules:
  0.0 98.8 jit_solution(18019687021531314662)
XLA Ops:
  0.0 3.9 %pack_other_core.7 = (bf16[4,128,640]{2,1,0:T(8,128)(2,1)}, s32[1]{0:T(128)}) custom-call(s32[128]{0:T(128)} %count_ref.1, s32[48]{0:T(128)} %ri_ref.1, s32[4,48]{1,0:T(4,128)} %mask_ref.1, bf16[128,6144]{1,0:T(8,128)(2,1)} %x_ref.1), custom_call_target="tpu_custom_call" | custom-call | flops 503316480 | bytes 1769472 | tf_op jit(solution)/shard_map/pack_other_core/pallas_call | solution.py:144
  4.5 93.1 %conditional.3 = (bf16[1024,768]{1,0:T(8,128)(2,1)S(1)}) conditional(s32[]{:T(128)} %convert_element_type.9, (s32[]{:T(128)}, s32[128]{0:T(128)}, s32[32,16]{0,1:T(8,128)}, bf16[1024,512]{1,0:T(8,128)(2,1)}, s32[48]{0:T(128)}, /*index=5*/s32[4,48]{1,0:T(4,128)}, bf16[128,6144]{1,0:T(8,128)(2,1)}) %tuple.58, (s32[128]{0:T(128)}, s32[32,16]{0,1:T(8,128)}, ...), branch_computations={%region_0.0_spmd, %region_5.0_spmd} | conditional | flops 14092861440 | bytes 89402104 | solution.py:467
  6.1 3.7 %pack_density.7.refs_0_ = bf16[768,384]{1,0:T(8,128)(2,1)S(1)} custom-call(s32[128]{0:T(128)} %get-tuple-element.179.count_ref, s32[32,16]{1,0:T(8,128)S(1)} %copy.10.mask_ref, bf16[1024,512]{1,0:T(8,128)(2,1)} %get-tuple-element.182.x_ref), custom_call_target="tpu_custom_call" | custom-call | flops 1006632960 | bytes 1048576 | tf_op jit(solution)/shard_map/cond/branch_1_fun/pack_density/pallas_call | solution.py:187
  10.0 2.2 %pack_own_core.7 = (bf16[256,640]{1,0:T(8,128)(2,1)S(1)}, bf16[256,640]{1,0:T(8,128)(2,1)S(1)}, bf16[256,640]{1,0:T(8,128)(2,1)S(1)}, bf16[256,640]{1,0:T(8,128)(2,1)S(1)}) custom-call(s32[128]{0:T(128)S(1)} %copy-done.12, s32[48]{0:T(128)S(1)} %copy-done.16, s32[4,48]{1,0:T(4,128)S(1)} %copy-done.8, bf16[128,6144]{1,0:T(8,128)(2,1)S(1)} %copy-done.3, ...), custom_call_target="tpu_custom_call" | custom-call | flops 503316480 | bytes 1769472 | tf_op jit(solution)/shard_map/cond/branch_1_fun/pack_own_core/pallas_call | solution.py:144
  12.2 3.0 %collective-permute-start.53 = (bf16[256,640]{1,0:T(8,128)(2,1)S(1)}, bf16[256,640]{1,0:T(8,128)(2,1)S(1)}, u32[]{:S(2)}, u32[]{:S(2)}) collective-permute-start(bf16[256,640]{1,0:T(8,128)(2,1)S(1)} %get-tuple-element.189), channel_id=1, source_target_pairs={{0,2},{1,3},{2,0},{3,1},{4,6},{5,7},{6,4},{7,5},{8,10},{9,11},{10,... | collective-permute-start | bytes 983048 | tf_op jit(solution)/shard_map/cond/branch_1_fun/ppermute | solution.py:233
  15.2 2.6 %collective-permute-start.56 = (bf16[256,640]{1,0:T(8,128)(2,1)S(1)}, bf16[256,640]{1,0:T(8,128)(2,1)S(1)}, u32[]{:S(2)}, u32[]{:S(2)}) collective-permute-start(bf16[256,640]{1,0:T(8,128)(2,1)S(1)} %get-tuple-element.191), channel_id=1, source_target_pairs={{0,4},{1,5},{2,6},{3,7},{4,0},{5,1},{6,2},{7,3},{8,12},{9,13},{10,... | collective-permute-start | bytes 983048 | tf_op jit(solution)/shard_map/cond/branch_1_fun/ppermute | solution.py:233
  17.8 11.8 %collective-permute-done.53.refs_1_ = bf16[256,640]{1,0:T(8,128)(2,1)S(1)} collective-permute-done((bf16[256,640]{1,0:T(8,128)(2,1)S(1)}, bf16[256,640]{1,0:T(8,128)(2,1)S(1)}, u32[]{:S(2)}, u32[]{:S(2)}) %collective-permute-start.53) | collective-permute-done | bytes 327712 | tf_op jit(solution)/shard_map/cond/branch_1_fun/ppermute | solution.py:233
  30.8 1.7 %collective-permute-start.58 = (bf16[384,640]{1,0:T(8,128)(2,1)S(1)}, bf16[384,640]{1,0:T(8,128)(2,1)S(1)}, u32[]{:S(2)}, u32[]{:S(2)}) collective-permute-start(bf16[384,640]{1,0:T(8,128)(2,1)S(1)} %pack_part.14.refs_4_), channel_id=1, source_target_pairs={{0,8},{8,0},{16,24},{24,16},{1,9},{9,1},{17,25},{25,17},{2,10},{10... | collective-permute-start | bytes 1474568 | tf_op jit(solution)/shard_map/cond/branch_1_fun/ppermute | solution.py:233
  32.5 1.5 %collective-permute-start.59 = (bf16[384,640]{1,0:T(8,128)(2,1)S(1)}, bf16[384,640]{1,0:T(8,128)(2,1)S(1)}, u32[]{:S(2)}, u32[]{:S(2)}) collective-permute-start(bf16[384,640]{1,0:T(8,128)(2,1)S(1)} %pack_part.14.refs_4_), channel_id=1, source_target_pairs={{0,16},{8,24},{16,0},{24,8},{1,17},{9,25},{17,1},{25,9},{2,18},{10... | collective-permute-start | bytes 1474568 | tf_op jit(solution)/shard_map/cond/branch_1_fun/ppermute | solution.py:233
  34.0 6.8 %collective-permute-done.56.refs_0_ = bf16[256,640]{1,0:T(8,128)(2,1)S(1)} collective-permute-done((bf16[256,640]{1,0:T(8,128)(2,1)S(1)}, bf16[256,640]{1,0:T(8,128)(2,1)S(1)}, u32[]{:S(2)}, u32[]{:S(2)}) %collective-permute-start.56) | collective-permute-done | bytes 327712 | tf_op jit(solution)/shard_map/cond/branch_1_fun/ppermute | solution.py:233
  42.0 1.6 %collective-permute-done.58.refs_6_ = bf16[384,640]{1,0:T(8,128)(2,1)S(1)} collective-permute-done((bf16[384,640]{1,0:T(8,128)(2,1)S(1)}, bf16[384,640]{1,0:T(8,128)(2,1)S(1)}, u32[]{:S(2)}, u32[]{:S(2)}) %collective-permute-start.58) | collective-permute-done | bytes 491552 | tf_op jit(solution)/shard_map/cond/branch_1_fun/ppermute | solution.py:233
  44.6 4.9 %collective-permute-start.64 = (bf16[768,384]{1,0:T(8,128)(2,1)S(1)}, bf16[768,384]{1,0:T(8,128)(2,1)S(1)}, u32[]{:S(2)}, u32[]{:S(2)}) collective-permute-start(bf16[768,384]{1,0:T(8,128)(2,1)S(1)} %pack_density.7.refs_0_), channel_id=1, source_target_pairs={{0,4},{1,5},{2,6},{3,7},{4,0},{5,1},{6,2},{7,3},{8,12},{9,13},{10,... | collective-permute-start | bytes 1769480 | tf_op jit(solution)/shard_map/cond/branch_1_fun/ppermute | solution.py:233
  49.6 1.5 %collective-permute-start.61 = (bf16[384,640]{1,0:T(8,128)(2,1)S(1)}, bf16[384,640]{1,0:T(8,128)(2,1)S(1)}, u32[]{:S(2)}, u32[]{:S(2)}) collective-permute-start(bf16[384,640]{1,0:T(8,128)(2,1)S(1)} %pack_part.15.refs_5_), channel_id=1, source_target_pairs={{0,16},{8,24},{16,0},{24,8},{1,17},{9,25},{17,1},{25,9},{2,18},{10... | collective-permute-start | bytes 1474568 | tf_op jit(solution)/shard_map/cond/branch_1_fun/ppermute | solution.py:233
  51.1 4.5 %collective-permute-done.54.refs_2_ = bf16[768,384]{1,0:T(8,128)(2,1)S(1)} collective-permute-done((bf16[768,384]{1,0:T(8,128)(2,1)S(1)}, bf16[768,384]{1,0:T(8,128)(2,1)S(1)}, u32[]{:S(2)}, u32[]{:S(2)}) %collective-permute-start.54) | collective-permute-done | bytes 589856 | tf_op jit(solution)/shard_map/cond/branch_1_fun/ppermute | solution.py:233
  55.6 1.5 %collective-permute-start.60 = (bf16[384,640]{1,0:T(8,128)(2,1)S(1)}, bf16[384,640]{1,0:T(8,128)(2,1)S(1)}, u32[]{:S(2)}, u32[]{:S(2)}) collective-permute-start(bf16[384,640]{1,0:T(8,128)(2,1)S(1)} %pack_part.15.refs_5_), channel_id=1, source_target_pairs={{0,8},{8,0},{16,24},{24,16},{1,9},{9,1},{17,25},{25,17},{2,10},{10... | collective-permute-start | bytes 1474568 | tf_op jit(solution)/shard_map/cond/branch_1_fun/ppermute | solution.py:233
  57.0 4.4 %collective-permute-done.61.refs_9_ = bf16[384,640]{1,0:T(8,128)(2,1)S(1)} collective-permute-done((bf16[384,640]{1,0:T(8,128)(2,1)S(1)}, bf16[384,640]{1,0:T(8,128)(2,1)S(1)}, u32[]{:S(2)}, u32[]{:S(2)}) %collective-permute-start.61) | collective-permute-done | bytes 491552 | tf_op jit(solution)/shard_map/cond/branch_1_fun/ppermute | solution.py:233
  61.4 1.5 %collective-permute-start.62 = (bf16[384,640]{1,0:T(8,128)(2,1)S(1)}, bf16[384,640]{1,0:T(8,128)(2,1)S(1)}, u32[]{:S(2)}, u32[]{:S(2)}) collective-permute-start(bf16[384,640]{1,0:T(8,128)(2,1)S(1)} %collective-permute-done.58.refs_6_), channel_id=1, source_target_pairs={{0,16},{8,24},{16,0},{24,8},{1,17},{9,25},{17,1},{25,9},{2,18},{10... | collective-permute-start | bytes 1474568 | tf_op jit(solution)/shard_map/cond/branch_1_fun/ppermute | solution.py:233
  62.9 1.5 %collective-permute-start.63 = (bf16[384,640]{1,0:T(8,128)(2,1)S(1)}, bf16[384,640]{1,0:T(8,128)(2,1)S(1)}, u32[]{:S(2)}, u32[]{:S(2)}) collective-permute-start(bf16[384,640]{1,0:T(8,128)(2,1)S(1)} %collective-permute-done.61.refs_9_), channel_id=1, source_target_pairs={{0,8},{8,0},{16,24},{24,16},{1,9},{9,1},{17,25},{25,17},{2,10},{10... | collective-permute-start | bytes 1474568 | tf_op jit(solution)/shard_map/cond/branch_1_fun/ppermute | solution.py:233
  64.4 10.3 %collective-permute-done.64.refs_0_ = bf16[768,384]{1,0:T(8,128)(2,1)S(1)} collective-permute-done((bf16[768,384]{1,0:T(8,128)(2,1)S(1)}, bf16[768,384]{1,0:T(8,128)(2,1)S(1)}, u32[]{:S(2)}, u32[]{:S(2)}) %collective-permute-start.64) | collective-permute-done | bytes 589856 | tf_op jit(solution)/shard_map/cond/branch_1_fun/ppermute | solution.py:233
  74.8 4.4 %collective-permute-done.63.refs_11_ = bf16[384,640]{1,0:T(8,128)(2,1)S(1)} collective-permute-done((bf16[384,640]{1,0:T(8,128)(2,1)S(1)}, bf16[384,640]{1,0:T(8,128)(2,1)S(1)}, u32[]{:S(2)}, u32[]{:S(2)}) %collective-permute-start.63) | collective-permute-done | bytes 491552 | tf_op jit(solution)/shard_map/cond/branch_1_fun/ppermute | solution.py:233
  79.2 7.5 %contract_near.7 = (f32[768,640]{1,0:T(8,128)S(1)}, bf16[1024,768]{1,0:T(8,128)(2,1)S(1)}, bf16[640,768]{1,0:T(8,128)(2,1)S(1)}, bf16[4,384,640]{2,1,0:T(8,128)(2,1)S(1)}) custom-call(s32[128]{0:T(128)S(1)} %copy-done.12, s32[48]{0:T(128)S(1)} %copy-done.16, bf16[768,384]{1,0:T(8,128)(2,1)S(1)} %pack_density.7.refs_0_, ...), custom_call_target="tpu_custom_call" | custom-call | flops 1509949440 | bytes 4325376 | tf_op jit(solution)/shard_map/cond/branch_1_fun/contract_near/pallas_call | solution.py:317
  88.0 2.5 %collective-permute-done.66.refs_0_ = bf16[768,384]{1,0:T(8,128)(2,1)S(1)} collective-permute-done((bf16[768,384]{1,0:T(8,128)(2,1)S(1)}, bf16[768,384]{1,0:T(8,128)(2,1)S(1)}, u32[]{:S(2)}, u32[]{:S(2)}) %collective-permute-start.66) | collective-permute-done | bytes 589856 | tf_op jit(solution)/shard_map/cond/branch_1_fun/ppermute | solution.py:233
  90.5 2.0 %collective-permute-done.67.refs_1_ = bf16[768,384]{1,0:T(8,128)(2,1)S(1)} collective-permute-done((bf16[768,384]{1,0:T(8,128)(2,1)S(1)}, bf16[768,384]{1,0:T(8,128)(2,1)S(1)}, u32[]{:S(2)}, u32[]{:S(2)}) %collective-permute-start.67) | collective-permute-done | bytes 589856 | tf_op jit(solution)/shard_map/cond/branch_1_fun/ppermute | solution.py:233
  92.5 5.1 %contract_last.7 = bf16[1024,768]{1,0:T(8,128)(2,1)S(1)} custom-call(f32[768,640]{1,0:T(8,128)S(1)} %contract_far.7.before, bf16[4,384,640]{2,1,0:T(8,128)(2,1)S(1)} %get-tuple-element.197.s_ref, bf16[1024,768]{1,0:T(8,128)(2,1)S(1)} %get-tuple-element.199.lam_hot, bf16[640,768]{1,0:T(8,128)(2,1)S(1)} %get-tuple-element.200.col_hot, ...), custom_call_target="tpu_custom_call" | custom-call | flops 754974720 | bytes 2162688 | tf_op jit(solution)/shard_map/cond/branch_1_fun/contract_last/pallas_call | solution.py:383
  (30 shorter events, 7.4 us)
Async XLA Ops:
  4.7 5.2 %copy-start.3 = (bf16[128,6144]{1,0:T(8,128)(2,1)S(1)}, bf16[128,6144]{1,0:T(8,128)(2,1)}, u32[]{:S(2)}) copy-start(bf16[128,6144]{1,0:T(8,128)(2,1)} %get-tuple-element.184.x_ref) | copy-start | bytes 4718596 | tf_op jit(solution)/shard_map/cond
  4.7 5.2 %copy-start.8 = (s32[4,48]{1,0:T(4,128)S(1)}, s32[4,48]{1,0:T(4,128)}, u32[]{:S(2)}) copy-start(s32[4,48]{1,0:T(4,128)} %get-tuple-element.183.mask_ref) | copy-start | bytes 2308 | tf_op jit(solution)/shard_map/cond
  4.8 5.2 %copy-start.12 = (s32[128]{0:T(128)S(1)}, s32[128]{0:T(128)}, u32[]{:S(2)}) copy-start(s32[128]{0:T(128)} %get-tuple-element.179.count_ref) | copy-start | bytes 1540 | tf_op jit(solution)/shard_map/cond
  4.8 5.2 %copy-start.16 = (s32[48]{0:T(128)S(1)}, s32[48]{0:T(128)}, u32[]{:S(2)}) copy-start(s32[48]{0:T(128)} %get-tuple-element.180.ri_ref) | copy-start | bytes 580 | tf_op jit(solution)/shard_map/cond
  4.8 5.2 %collective-permute-start.51 = (bf16[4,128,640]{2,1,0:T(8,128)(2,1)}, bf16[4,128,640]{2,1,0:T(8,128)(2,1)S(1)}, u32[]{:S(2)}, u32[]{:S(2)}) collective-permute-start(bf16[4,128,640]{2,1,0:T(8,128)(2,1)} %get-tuple-element.185), channel_id=1, source_target_pairs={{0,1},{1,0},{2,3},{3,2},{4,5},{5,4},{6,7},{7,6},{8,9},{9,8},{10,11... | collective-permute-start | bytes 1966088 | tf_op jit(solution)/shard_map/cond/branch_1_fun/ppermute | solution.py:233
  9.7 8.1 %collective-permute-start.52 = (bf16[768,384]{1,0:T(8,128)(2,1)S(1)}, bf16[768,384]{1,0:T(8,128)(2,1)S(1)}, u32[]{:S(2)}, u32[]{:S(2)}) collective-permute-start(bf16[768,384]{1,0:T(8,128)(2,1)S(1)} %pack_density.7.refs_0_), channel_id=1, source_target_pairs={{0,1},{1,0},{2,3},{3,2},{4,5},{5,4},{6,7},{7,6},{8,9},{9,8},{10,11... | collective-permute-start | bytes 1769480 | tf_op jit(solution)/shard_map/cond/branch_1_fun/ppermute | solution.py:233
  12.2 17.4 %collective-permute-start.53 = (bf16[256,640]{1,0:T(8,128)(2,1)S(1)}, bf16[256,640]{1,0:T(8,128)(2,1)S(1)}, u32[]{:S(2)}, u32[]{:S(2)}) collective-permute-start(bf16[256,640]{1,0:T(8,128)(2,1)S(1)} %get-tuple-element.189), channel_id=1, source_target_pairs={{0,2},{1,3},{2,0},{3,1},{4,6},{5,7},{6,4},{7,5},{8,10},{9,11},{10,... | collective-permute-start | bytes 983048 | tf_op jit(solution)/shard_map/cond/branch_1_fun/ppermute | solution.py:233
  15.2 25.6 %collective-permute-start.56 = (bf16[256,640]{1,0:T(8,128)(2,1)S(1)}, bf16[256,640]{1,0:T(8,128)(2,1)S(1)}, u32[]{:S(2)}, u32[]{:S(2)}) collective-permute-start(bf16[256,640]{1,0:T(8,128)(2,1)S(1)} %get-tuple-element.191), channel_id=1, source_target_pairs={{0,4},{1,5},{2,6},{3,7},{4,0},{5,1},{6,2},{7,3},{8,12},{9,13},{10,... | collective-permute-start | bytes 983048 | tf_op jit(solution)/shard_map/cond/branch_1_fun/ppermute | solution.py:233
  17.8 23.0 %collective-permute-start.57 = (bf16[256,640]{1,0:T(8,128)(2,1)S(1)}, bf16[256,640]{1,0:T(8,128)(2,1)S(1)}, u32[]{:S(2)}, u32[]{:S(2)}) collective-permute-start(bf16[256,640]{1,0:T(8,128)(2,1)S(1)} %get-tuple-element.192), channel_id=1, source_target_pairs={{0,6},{1,7},{2,4},{3,5},{4,2},{5,3},{6,0},{7,1},{8,14},{9,15},{10,... | collective-permute-start | bytes 983048 | tf_op jit(solution)/shard_map/cond/branch_1_fun/ppermute | solution.py:233
  30.8 12.8 %collective-permute-start.58 = (bf16[384,640]{1,0:T(8,128)(2,1)S(1)}, bf16[384,640]{1,0:T(8,128)(2,1)S(1)}, u32[]{:S(2)}, u32[]{:S(2)}) collective-permute-start(bf16[384,640]{1,0:T(8,128)(2,1)S(1)} %pack_part.14.refs_4_), channel_id=1, source_target_pairs={{0,8},{8,0},{16,24},{24,16},{1,9},{9,1},{17,25},{25,17},{2,10},{10... | collective-permute-start | bytes 1474568 | tf_op jit(solution)/shard_map/cond/branch_1_fun/ppermute | solution.py:233
  32.5 12.1 %collective-permute-start.59 = (bf16[384,640]{1,0:T(8,128)(2,1)S(1)}, bf16[384,640]{1,0:T(8,128)(2,1)S(1)}, u32[]{:S(2)}, u32[]{:S(2)}) collective-permute-start(bf16[384,640]{1,0:T(8,128)(2,1)S(1)} %pack_part.14.refs_4_), channel_id=1, source_target_pairs={{0,16},{8,24},{16,0},{24,8},{1,17},{9,25},{17,1},{25,9},{2,18},{10... | collective-permute-start | bytes 1474568 | tf_op jit(solution)/shard_map/cond/branch_1_fun/ppermute | solution.py:233
  34.0 21.5 %collective-permute-start.54 = (bf16[768,384]{1,0:T(8,128)(2,1)S(1)}, bf16[768,384]{1,0:T(8,128)(2,1)S(1)}, u32[]{:S(2)}, u32[]{:S(2)}) collective-permute-start(bf16[768,384]{1,0:T(8,128)(2,1)S(1)} %pack_density.7.refs_0_), channel_id=1, source_target_pairs={{0,2},{1,3},{2,0},{3,1},{4,6},{5,7},{6,4},{7,5},{8,10},{9,11},{10,... | collective-permute-start | bytes 1769480 | tf_op jit(solution)/shard_map/cond/branch_1_fun/ppermute | solution.py:233
  44.6 30.1 %collective-permute-start.64 = (bf16[768,384]{1,0:T(8,128)(2,1)S(1)}, bf16[768,384]{1,0:T(8,128)(2,1)S(1)}, u32[]{:S(2)}, u32[]{:S(2)}) collective-permute-start(bf16[768,384]{1,0:T(8,128)(2,1)S(1)} %pack_density.7.refs_0_), channel_id=1, source_target_pairs={{0,4},{1,5},{2,6},{3,7},{4,0},{5,1},{6,2},{7,3},{8,12},{9,13},{10,... | collective-permute-start | bytes 1769480 | tf_op jit(solution)/shard_map/cond/branch_1_fun/ppermute | solution.py:233
  49.6 11.8 %collective-permute-start.61 = (bf16[384,640]{1,0:T(8,128)(2,1)S(1)}, bf16[384,640]{1,0:T(8,128)(2,1)S(1)}, u32[]{:S(2)}, u32[]{:S(2)}) collective-permute-start(bf16[384,640]{1,0:T(8,128)(2,1)S(1)} %pack_part.15.refs_5_), channel_id=1, source_target_pairs={{0,16},{8,24},{16,0},{24,8},{1,17},{9,25},{17,1},{25,9},{2,18},{10... | collective-permute-start | bytes 1474568 | tf_op jit(solution)/shard_map/cond/branch_1_fun/ppermute | solution.py:233
  55.6 19.2 %collective-permute-start.60 = (bf16[384,640]{1,0:T(8,128)(2,1)S(1)}, bf16[384,640]{1,0:T(8,128)(2,1)S(1)}, u32[]{:S(2)}, u32[]{:S(2)}) collective-permute-start(bf16[384,640]{1,0:T(8,128)(2,1)S(1)} %pack_part.15.refs_5_), channel_id=1, source_target_pairs={{0,8},{8,0},{16,24},{24,16},{1,9},{9,1},{17,25},{25,17},{2,10},{10... | collective-permute-start | bytes 1474568 | tf_op jit(solution)/shard_map/cond/branch_1_fun/ppermute | solution.py:233
  57.0 17.7 %collective-permute-start.55 = (bf16[768,384]{1,0:T(8,128)(2,1)S(1)}, bf16[768,384]{1,0:T(8,128)(2,1)S(1)}, u32[]{:S(2)}, u32[]{:S(2)}) collective-permute-start(bf16[768,384]{1,0:T(8,128)(2,1)S(1)} %collective-permute-done.54.refs_2_), channel_id=1, source_target_pairs={{0,1},{1,0},{2,3},{3,2},{4,5},{5,4},{6,7},{7,6},{8,9},{9,8},{10,11... | collective-permute-start | bytes 1769480 | tf_op jit(solution)/shard_map/cond/branch_1_fun/ppermute | solution.py:233
  61.4 13.4 %collective-permute-start.62 = (bf16[384,640]{1,0:T(8,128)(2,1)S(1)}, bf16[384,640]{1,0:T(8,128)(2,1)S(1)}, u32[]{:S(2)}, u32[]{:S(2)}) collective-permute-start(bf16[384,640]{1,0:T(8,128)(2,1)S(1)} %collective-permute-done.58.refs_6_), channel_id=1, source_target_pairs={{0,16},{8,24},{16,0},{24,8},{1,17},{9,25},{17,1},{25,9},{2,18},{10... | collective-permute-start | bytes 1474568 | tf_op jit(solution)/shard_map/cond/branch_1_fun/ppermute | solution.py:233
  62.9 16.3 %collective-permute-start.63 = (bf16[384,640]{1,0:T(8,128)(2,1)S(1)}, bf16[384,640]{1,0:T(8,128)(2,1)S(1)}, u32[]{:S(2)}, u32[]{:S(2)}) collective-permute-start(bf16[384,640]{1,0:T(8,128)(2,1)S(1)} %collective-permute-done.61.refs_9_), channel_id=1, source_target_pairs={{0,8},{8,0},{16,24},{24,16},{1,9},{9,1},{17,25},{25,17},{2,10},{10... | collective-permute-start | bytes 1474568 | tf_op jit(solution)/shard_map/cond/branch_1_fun/ppermute | solution.py:233
  74.8 11.9 %collective-permute-start.65 = (bf16[768,384]{1,0:T(8,128)(2,1)S(1)}, bf16[768,384]{1,0:T(8,128)(2,1)S(1)}, u32[]{:S(2)}, u32[]{:S(2)}) collective-permute-start(bf16[768,384]{1,0:T(8,128)(2,1)S(1)} %collective-permute-done.64.refs_0_), channel_id=1, source_target_pairs={{0,1},{1,0},{2,3},{3,2},{4,5},{5,4},{6,7},{7,6},{8,9},{9,8},{10,11... | collective-permute-start | bytes 1769480 | tf_op jit(solution)/shard_map/cond/branch_1_fun/ppermute | solution.py:233
  74.8 15.7 %collective-permute-start.66 = (bf16[768,384]{1,0:T(8,128)(2,1)S(1)}, bf16[768,384]{1,0:T(8,128)(2,1)S(1)}, u32[]{:S(2)}, u32[]{:S(2)}) collective-permute-start(bf16[768,384]{1,0:T(8,128)(2,1)S(1)} %collective-permute-done.64.refs_0_), channel_id=1, source_target_pairs={{0,2},{1,3},{2,0},{3,1},{4,6},{5,7},{6,4},{7,5},{8,10},{9,11},{10,... | collective-permute-start | bytes 1769480 | tf_op jit(solution)/shard_map/cond/branch_1_fun/ppermute | solution.py:233
  90.5 2.0 %collective-permute-start.67 = (bf16[768,384]{1,0:T(8,128)(2,1)S(1)}, bf16[768,384]{1,0:T(8,128)(2,1)S(1)}, u32[]{:S(2)}, u32[]{:S(2)}) collective-permute-start(bf16[768,384]{1,0:T(8,128)(2,1)S(1)} %collective-permute-done.66.refs_0_), channel_id=1, source_target_pairs={{0,1},{1,0},{2,3},{3,2},{4,5},{5,4},{6,7},{7,6},{8,9},{9,8},{10,11... | collective-permute-start | bytes 1769480 | tf_op jit(solution)/shard_map/cond/branch_1_fun/ppermute | solution.py:233
  97.6 1.1 %copy-start.4 = (bf16[1024,768]{1,0:T(8,128)(2,1)}, bf16[1024,768]{1,0:T(8,128)(2,1)S(1)}, u32[]{:S(2)}) copy-start(bf16[1024,768]{1,0:T(8,128)(2,1)S(1)} %get-tuple-element.360) | copy-start | bytes 4718596
where the time goes:
time: 99 us; the launch traced here: 98.8 us
  waiting for transfers between devices  49.3 us (50%)
  Pallas kernels  26 us (26%)
  starting transfers between devices  20.5 us (21%)
  local copies, waits for them, and re-layouts  1.93 us (2%)
    ppermute x17, waiting for transfers between devices, exchange(): return lax.ppermute(x, axis, [(i, i ^ bit) for i in range(peers)])  49.3 us
    ppermute x17, starting transfers between devices, exchange(): return lax.ppermute(x, axis, [(i, i ^ bit) for i in range(peers)])  20.5 us
    pallas_call x1, Pallas kernels, contract_near(): pl.pallas_call(body, out_shape=[jax.ShapeDtypeStruct((lam, cols), F32), j...  7.45 us
    pallas_call x2, Pallas kernels, pack_integrals(): pl.pallas_call(body, out_shape=out_shape, in_specs=[SMEM_SPEC, SMEM_SPEC,...  6.07 us
    pallas_call x1, Pallas kernels, contract_last(): pl.pallas_call(body, out_shape=jax.ShapeDtypeStruct((rows, wide), BF16),...  5.08 us
    pallas_call x1, Pallas kernels, pack_density(): pl.pallas_call(body, out_shape=jax.ShapeDtypeStruct((lam_size, sum_size),...  3.66 us
    pallas_call x2, Pallas kernels, pack_part(): pl.pallas_call(body, out_shape=jax.ShapeDtypeStruct((size, cols), BF16),...  2.41 us
  transfers between devices with their start and end apart: 17, of which 10 were waited for; matrix products, arithmetic and copies ran while one was open for 1% of the time, Pallas kernels for 17%

commit v1 on v0

--- a/solution.py
+++ b/solution.py
@@ -9,6 +9,7 @@
 RW = 128
 CORES = 2
 VMEM = 48 * 1024 * 1024
+TILE = 256
 BF16 = jnp.bfloat16
 F32 = jnp.float32
 SMEM_SPEC = pl.BlockSpec(memory_space=pltpu.SMEM)
@@ -80,22 +81,31 @@
         lax.fori_loop(0, atoms, atom, jnp.int32(0))
 
 
-def first_fit(count_ref, ri_ref, groups, levels):
-    level = jnp.int32(0)
-    for axis, (ref, parts) in enumerate(zip((count_ref, count_ref, ri_ref), groups)):
-        per = ref.shape[0] // parts
-        most = jnp.int32(0)
-        for g in range(parts):
-            total = jnp.int32(0)
-            for i in range(per):
-                total = total + ref[g * per + i]
-            most = jnp.maximum(most, total)
-        for n, sizes in enumerate(levels[:-1]):
-            level = jnp.where(most > sizes[axis], jnp.maximum(level, n + 1), level)
-    return level
-
-
-def pack_integrals(tc, block_mask, basis_count, ri_count, ncols, packed, unroll, arrived=None, levels=None):
+def first_fit(basis_count, ri_count, groups, levels):
+    def body(count_ref, ri_ref, o_ref):
+        level = jnp.int32(0)
+        for axis, (ref, parts) in enumerate(zip((count_ref, count_ref, ri_ref), groups)):
+            per = ref.shape[0] // parts
+            most = jnp.int32(0)
+            for g in range(parts):
+                total = jnp.int32(0)
+                for i in range(per):
+                    total = total + ref[g * per + i]
+                most = jnp.maximum(most, total)
+            for n, sizes in enumerate(levels[:-1]):
+                level = jnp.where(most > sizes[axis], jnp.maximum(level, n + 1), level)
+        o_ref[0] = level
+
+    return pl.pallas_call(
+        body,
+        out_shape=jax.ShapeDtypeStruct((1,), jnp.int32),
+        in_specs=[SMEM_SPEC, SMEM_SPEC],
+        out_specs=SMEM_SPEC,
+        name="first_fit",
+    )(basis_count, ri_count)
+
+
+def pack_integrals(tc, block_mask, basis_count, ri_count, ncols, packed, unroll, arrived=None):
     rows, cols = tc.shape
     atoms = rows // BW
     wide = cols // ncols
@@ -104,8 +114,6 @@
     first = arrived is None
 
     def body(count_ref, ri_ref, mask_ref, x_ref, *refs):
-        if levels is not None:
-            refs[1][0] = first_fit(count_ref, ri_ref, *levels)
         outs = refs[:1] if first else refs[1 : 1 + chips]
         held, hot = refs[-2:] if first else refs[-3:-1]
         made = outs[0] if first else refs[-1]
@@ -138,9 +146,6 @@
     merged = jax.ShapeDtypeStruct((CORES * rows, packed), BF16)
     out_shape = [jax.ShapeDtypeStruct(shape, BF16)] if first else [merged] * chips
     out_specs = [VMEM_SPEC] * len(out_shape)
-    if levels is not None:
-        out_shape.append(jax.ShapeDtypeStruct((1,), jnp.int32))
-        out_specs.append(SMEM_SPEC)
     return pl.pallas_call(
         body,
         out_shape=out_shape,
@@ -161,9 +166,11 @@
     tile = rows // steps
     out_tile = lam_size // steps
 
-    def body(count_ref, mask_ref, x_ref, o_ref, hot, keep, mid):
+    def body(count_ref, mask_ref, x_ref, o_ref, upper_ref, lower_ref, hot, keep, mid):
         row, col = lax.axis_index("row"), lax.axis_index("col")
-        of_atom = ones_where(iota((sum_atoms, cols), 1) // BW == iota((sum_atoms, cols), 0))
+        first = iota((sum_atoms, cols), 0) * BW
+        lane = iota((sum_atoms, cols), 1)
+        of_atom = ones_where((lane >= first) & (lane < first + BW))
         keep[...] = jnp.dot(ones_where(mask_ref[...] > 0), of_atom, preferred_element_type=F32).astype(BF16)
         pack_cols(count_ref, col * sum_atoms, sum_atoms, BW, sum_size, hot, unroll)
 
@@ -171,7 +178,8 @@
         def _(i):
             at = span(i, tile)
             shape = (tile, lam_atoms)
-            atom = ones_where((iota(shape, 0) + i * tile) // BW == iota(shape, 1))
+            first = iota(shape, 1) * BW - i * tile
+            atom = ones_where((iota(shape, 0) >= first) & (iota(shape, 0) < first + BW))
             kept = jnp.dot(atom, keep[...], preferred_element_type=F32)
             x = jnp.where(kept > 0.5, x_ref[at, :].astype(F32), 0.0).astype(BF16)
             mid[at, :] = jnp.dot(x, hot[...], preferred_element_type=F32).astype(BF16)
@@ -184,11 +192,14 @@
             left = ones_where(iota((out_tile, rows), 0) + i * out_tile == place)
             o_ref[at, :] = jnp.dot(left, mid[...], preferred_element_type=F32).astype(BF16)
 
-    return pl.pallas_call(
-        body,
-        out_shape=jax.ShapeDtypeStruct((lam_size, sum_size), BF16),
+        upper_ref[...] = o_ref[pl.ds(0, TILE), :]
+        lower_ref[...] = o_ref[pl.ds(TILE, lam_size - TILE), :]
+
+    return pl.pallas_call(
+        body,
+        out_shape=[jax.ShapeDtypeStruct((n, sum_size), BF16) for n in (lam_size, TILE, lam_size - TILE)],
         in_specs=[SMEM_SPEC, VMEM_SPEC, VMEM_SPEC],
-        out_specs=VMEM_SPEC,
+        out_specs=[VMEM_SPEC] * 3,
         scratch_shapes=[
             pltpu.VMEM((cols, sum_size), BF16),
             pltpu.VMEM((lam_atoms, cols), BF16),
@@ -245,23 +256,21 @@
     return have
 
 
-def add_parts(total, tile, unroll, d_refs, sums, before=None):
+def add_parts(total, unroll, d_refs, sums, before=None):
     lam, cols = total.shape
 
-    @loop(lam // tile, unroll)
+    @loop(lam // TILE, unroll)
     def _(j):
-        out = span(j, tile)
+        out = span(j, TILE)
         x = None if before is None else before[out, :]
         for chunks, part in zip(d_refs, sums):
             if len(chunks) == 1:
                 d = chunks[0][out, :]
             elif isinstance(j, int):
-                size = chunks[0].shape[0]
-                d = chunks[j * tile // size][pl.ds(j * tile % size, tile), :]
+                d = chunks[0][...] if j == 0 else chunks[1][span(j - 1, TILE), :]
             else:
-                per = chunks[0].shape[0] // tile
-                inner = span(lax.rem(j, per), tile)
-                d = jnp.where(j < per, chunks[0][inner, :].astype(F32), chunks[1][inner, :].astype(F32)).astype(BF16)
+                d = chunks[1][span(jnp.maximum(j - 1, 0), TILE), :].astype(F32)
+                d = jnp.where(j == 0, chunks[0][...].astype(F32), d).astype(BF16)
             y = jnp.dot(d, part(), preferred_element_type=F32)
             x = y if x is None else x + y
         total[out, :] = x
@@ -279,51 +288,67 @@
     return [chunk for chunks in dens.values() for chunk in chunks]
 
 
-def contract_near(dens, integrals, basis_count, ri_count, ncols, rows, wide, unroll):
+def ways_back(basis_count, ri_count, nrows, ncols, rows, wide, lam, cols, unroll):
+    lam_atoms, blocks = rows // BW, wide // RW
+
+    def body(count_ref, ri_ref, lam_hot, col_hot):
+        row, col = lax.axis_index("row"), lax.axis_index("col")
+        pack_cols(count_ref, row * lam_atoms, lam_atoms, BW, lam, lam_hot, unroll)
+        place = place_row(ri_ref, col * blocks, blocks, RW)
+
+        @loop(cols // RW, unroll)
+        def _(i):
+            col_hot[span(i, RW), :] = ones_where(iota((RW, wide), 0) + i * RW == place)
+
+    return pl.pallas_call(
+        body,
+        out_shape=[jax.ShapeDtypeStruct((rows, lam), BF16), jax.ShapeDtypeStruct((cols, wide), BF16)],
+        in_specs=[SMEM_SPEC, SMEM_SPEC],
+        out_specs=[VMEM_SPEC] * 2,
+        compiler_params=params(16 * 1024 * 1024),
+        name="ways_back",
+    )(basis_count, ri_count)
+
+
+def contract_near(dens, integrals, ncols, unroll):
     lam, depth = dens[0][0].shape
     groups, nrows = len(integrals), len(integrals[0])
     sums = [integrals[g][far] for far in range(nrows) for g in range(groups)]
     cols = sums[0].shape[1]
-    lam_atoms, blocks = rows // BW, wide // RW
     n, parts = len(dens), len(sums)
 
-    def body(count_ref, ri_ref, *refs):
+    def body(*refs):
         d_refs, refs = split_refs(dens, refs)
         s_refs, refs = refs[:parts], refs[parts:]
-        total, lam_hot, col_hot, s_rest, s_all, s_sem, r_sem = refs
+        total, s_rest, s_all, s_sem, r_sem = refs
         row, col = lax.axis_index("row"), lax.axis_index("col")
         for j, ref in enumerate(s_refs):
             part = (row ^ (j // groups)) * groups + (col // (ncols // groups) ^ (j % groups))
             pltpu.make_async_copy(ref, s_all.at[part], s_sem.at[part]).start()
-        pack_cols(count_ref, row * lam_atoms, lam_atoms, BW, lam, lam_hot, unroll)
-        place = place_row(ri_ref, col * blocks, blocks, RW)
-
-        @loop(cols // RW, unroll)
-        def _(i):
-            col_hot[span(i, RW), :] = ones_where(iota((RW, wide), 0) + i * RW == place)
 
         @pl.loop(0, parts)
         def _(i):
             pltpu.make_async_copy(s_all.at[i], s_all.at[i], s_sem.at[i]).wait()
 
-        rest = [pltpu.make_async_copy(s_all.at[col ^ far], s_rest.at[far - n], r_sem.at[far - n]) for far in range(n, parts)]
+        rest = [
+            pltpu.make_async_copy(s_all.at[col ^ far], s_rest.at[far - n], r_sem.at[far - n])
+            for far in range(n, parts)
+        ]
         for copy in rest:
             copy.start()
-        add_parts(total, lam // 2, unroll, d_refs, [lambda far=far: s_all[col ^ far] for far in range(n)])
+        add_parts(total, unroll, d_refs, [lambda far=far: s_all[col ^ far] for far in range(n)])
         for copy in rest:
             copy.wait()
 
-    need = 2 * (n * depth * lam + 2 * parts * depth * cols + 4 * lam * cols + rows * lam + cols * wide)
+    need = 2 * (n * depth * lam + 2 * parts * depth * cols + 4 * lam * cols)
     return pl.pallas_call(
         body,
         out_shape=[
             jax.ShapeDtypeStruct((lam, cols), F32),
-            jax.ShapeDtypeStruct((rows, lam), BF16),
-            jax.ShapeDtypeStruct((cols, wide), BF16),
             jax.ShapeDtypeStruct((parts - n, depth, cols), BF16),
         ],
-        in_specs=[SMEM_SPEC, SMEM_SPEC] + [VMEM_SPEC] * n + [ANY_SPEC] * parts,
-        out_specs=[VMEM_SPEC] * 4,
+        in_specs=[VMEM_SPEC] * n + [ANY_SPEC] * parts,
+        out_specs=[VMEM_SPEC] * 2,
         scratch_shapes=[
             pltpu.VMEM((parts, depth, cols), BF16),
             pltpu.SemaphoreType.DMA((parts,)),
@@ -332,7 +357,7 @@
         compiler_params=params(need + 4 * 1024 * 1024),
         cost_estimate=cost(2 * n * depth * lam * cols, 2 * n * depth * (lam + cols)),
         name="contract_near",
-    )(basis_count, ri_count, *flat(dens), *sums)
+    )(*flat(dens), *sums)
 
 
 def contract_far(dens, first, total, sums, unroll):
@@ -341,7 +366,7 @@
 
     def body(before, s_ref, *refs):
         d_refs, (o_ref,) = split_refs(dens, refs)
-        add_parts(o_ref, lam // 2, unroll, d_refs, [lambda i=i: s_ref[first + i] for i in range(n)], before)
+        add_parts(o_ref, unroll, d_refs, [lambda i=i: s_ref[first + i] for i in range(n)], before)
 
     need = 2 * (n * depth * lam + sums.size + 4 * lam * cols)
     return pl.pallas_call(
@@ -362,35 +387,26 @@
     half = lam // 2
 
     def body(before, s_ref, lam_hot, col_hot, *refs):
-        d_refs, (o_ref, total, packed, made, sem) = split_refs(dens, refs)
-        add_parts(total, half, unroll, d_refs, [lambda i=i: s_ref[first + i] for i in range(n)], before)
+        d_refs, (o_ref, total, packed) = split_refs(dens, refs)
+        add_parts(total, unroll, d_refs, [lambda i=i: s_ref[first + i] for i in range(n)], before)
 
         @loop(2, unroll)
         def _(j):
             x = total[span(j, half), :].astype(BF16)
             packed[span(j, half), :] = jnp.dot(x, col_hot[...], preferred_element_type=F32).astype(BF16)
 
-        copies = []
-        for j in range(4):
+        @loop(4, unroll)
+        def _(j):
             out = span(j, rows // 4)
-            made[out, :] = jnp.dot(lam_hot[out, :], packed[...], preferred_element_type=F32).astype(BF16)
-            copies.append(pltpu.make_async_copy(made.at[out, :], o_ref.at[out, :], sem.at[j]))
-            copies[-1].start()
-        for copy in copies:
-            copy.wait()
+            o_ref[out, :] = jnp.dot(lam_hot[out, :], packed[...], preferred_element_type=F32).astype(BF16)
 
     need = 2 * (n * depth * lam + sums.size + 4 * lam * cols + rows * lam + cols * wide + (lam + rows) * wide)
     return pl.pallas_call(
         body,
         out_shape=jax.ShapeDtypeStruct((rows, wide), BF16),
         in_specs=[VMEM_SPEC] * (4 + len(flat(dens))),
-        out_specs=ANY_SPEC,
-        scratch_shapes=[
-            pltpu.VMEM((lam, cols), F32),
-            pltpu.VMEM((lam, wide), BF16),
-            pltpu.VMEM((rows, wide), BF16),
-            pltpu.SemaphoreType.DMA((4,)),
-        ],
+        out_specs=VMEM_SPEC,
+        scratch_shapes=[pltpu.VMEM((lam, cols), F32), pltpu.VMEM((lam, wide), BF16)],
         compiler_params=params(need + 4 * 1024 * 1024),
         cost_estimate=cost(2 * n * depth * lam * cols, 2 * n * depth * (lam + cols)),
         name="contract_last",
@@ -400,7 +416,7 @@
 def program(lam_size, sum_size, col_size, common):
     unroll = common
 
-    def run(three_center, density, block_mask, density_mask, basis_count, ri_count, other):
+    def run(three_center, density, block_mask, density_mask, basis_count, ri_count):
         ncols = lax.axis_size("col")
         nrows = lax.axis_size("row")
         chips = ncols // CORES
@@ -411,32 +427,38 @@
         far_bit, near_bits = chip_bits[0], chip_bits[1:]
 
         counts = (block_mask, basis_count, ri_count, ncols, col_size, unroll)
-        if not common:
-            other = pack_integrals(three_center, *counts)[0]
-        other = exchange(other, "col", 1)
-        own = pack_density(density, density_mask, basis_count, lam_size, sum_size, unroll)
+        other = exchange(pack_integrals(three_center, *counts)[0], "col", 1)
+        own, upper, lower = pack_density(density, density_mask, basis_count, lam_size, sum_size, unroll)
+        lines = [{0: upper, far_bit: exchange(upper, "col", far_bit)}, {0: lower}]
         near = {0: own, 1: exchange(own, "col", 1)}
         pieces = pack_integrals(three_center, *counts, after(other, own))
+        early = lines[0][far_bit]
         got = [pieces[0]] + [exchange(pieces[t], "col", CORES * t) for t in range(1, chips)]
         per = depth // pieces[0].shape[0]
+        lam_hot, col_hot = ways_back(
+            basis_count, ri_count, nrows, ncols, rows, wide, lam_size, col_size, unroll
+        )
         parts, groups, orders = [], [], []
         for g in range(chips // per):
             arrived = got[g * per : (g + 1) * per]
             if g == 0:
-                arrived = [after(arrived[0], near[1])] + arrived[1:]
+                arrived = [after(arrived[0], near[1], early)] + arrived[1:]
+            elif g == 1:
+                arrived = [after(arrived[0], lam_hot)] + arrived[1:]
             part = pack_part(arrived, basis_count, g * per, ncols, sum_size)
             if g == 0:
-                near.update(double(after(own, part), "col", near_bits))
-                steps = [near[far] for far in near if far > 1]
+                forward = double(after(early, part), "col", near_bits)
+                lines[0].update({far_bit | far: block for far, block in forward.items()})
             else:
-                part = after(part, *[groups[0][bit] for bit in row_bits])
+                part = after(part, *[groups[0][bit] for bit in row_bits], lines[0][ncols - CORES])
             parts.append(part)
             orders.append(row_bits if g % 2 == 0 else row_bits[::-1])
             groups.append({0: part})
-            for i, bit in enumerate(orders[g]):
-                groups[g][bit] = exchange(after(part, *steps) if g > 0 and i > 0 else part, "row", bit)
+            for bit in orders[g]:
+                groups[g][bit] = exchange(part, "row", bit)
         step = groups[-1][orders[-1][0]]
-        line = {0: own, far_bit: exchange(after(own, parts[-1]), "col", far_bit)}
+        lines[1][far_bit] = exchange(after(lower, parts[-1]), "col", far_bit)
+        near.update(double(after(own, parts[-1]), "col", near_bits))
         for g, have in enumerate(groups):
             done = [0, orders[g][0]]
             for bit in orders[g][1:]:
@@ -446,18 +468,17 @@
         for far in [far for far in near if far > 1]:
             near[far | 1] = exchange(near[far], "col", 1)
         first = {far: [near[far]] for far in sorted(near)}
-        total, lam_hot, col_hot, sums = contract_near(
-            first, groups, basis_count, ri_count, ncols, rows, wide, unroll
-        )
-        for away, block in double(line[far_bit], "col", near_bits).items():
-            line[far_bit | away] = block
+        total, sums = contract_near(first, groups, ncols, unroll)
+        for away, block in double(lines[1][far_bit], "col", near_bits).items():
+            lines[1][far_bit | away] = block
         middle = {}
         for far in range(far_bit, ncols - CORES, CORES):
-            middle[far] = [line[far]]
-            middle[far | 1] = [exchange(line[far], "col", 1)]
+            middle[far] = [line[far] for line in lines]
+            middle[far | 1] = [exchange(line[far], "col", 1) for line in lines]
         total = contract_far(middle, 0, total, sums, unroll)
-        end = line[ncols - CORES]
-        last = {ncols - CORES: [end], ncols - 1: [exchange(after(end, total), "col", 1)]}
+        ends = [line[ncols - CORES] for line in lines]
+        last = {ncols - CORES: ends}
+        last[ncols - 1] = [exchange(ends[0], "col", 1), exchange(after(ends[1], total), "col", 1)]
         return contract_last(last, len(middle), total, sums, lam_hot, col_hot, unroll)
 
     return run
@@ -478,17 +499,8 @@
         (rows * 3 // 4, depth, wide),
         (rows, depth, wide),
     )
-    other, level = pack_integrals(
-        three_center,
-        block_mask,
-        basis_count,
-        ri_count,
-        ncols,
-        levels[0][2],
-        True,
-        levels=((nrows, ncols, ncols), levels),
-    )
-    args = (three_center, density, block_mask, density_mask, basis_count, ri_count, other)
+    level = first_fit(basis_count, ri_count, (nrows, ncols, ncols), levels)
+    args = (three_center, density, block_mask, density_mask, basis_count, ri_count)
     run = program(*levels[-1], False)
     for n in reversed(range(len(levels) - 1)):
         run = choose(level[0] == n, program(*levels[n], n == 0), run)

time: 99 us -> 108 us (1.091)
  starting transfers between devices: 20.5 us -> 26 us
  waiting for transfers between devices: 49.3 us -> 53.9 us
    ppermute x17 -> x21, starting transfers between devices: 20.5 us -> 26 us  [exchange(): return lax.ppermute(x, axis, [(i, i ^ bit) for i in range(peers)])]
    ppermute x17 -> x21, waiting for transfers between devices: 49.3 us -> 53.9 us  [exchange(): return lax.ppermute(x, axis, [(i, i ^ bit) for i in range(peers)])]
    pallas_call x1 -> x3, Pallas kernels: 3.66 us -> 6.44 us  [the longest x1 4.05 us: pack_density(): pl.pallas_call(body, out_shape=[jax.ShapeDtypeStruct((n, sum_size), BF16)...]
    pallas_call x1, Pallas kernels: 5.08 us -> 3.42 us  [contract_last(): pl.pallas_call(body, out_shape=jax.ShapeDtypeStruct((rows, wide), BF16),...]
  transfers between devices with their start and end apart: 17 -> 21, of which waited for: 10 -> 8; matrix products, arithmetic and copies ran while one was open for 1% -> 0% of each run, Pallas kernels for 17% -> 16%
where the time goes in v1:
time: 108 us
  waiting for transfers between devices  53.9 us (50%)
  starting transfers between devices  26 us (24%)
  Pallas kernels  25.2 us (23%)
  local copies, waits for them, and re-layouts  1.24 us (1%)
    ppermute x21, waiting for transfers between devices, exchange(): return lax.ppermute(x, axis, [(i, i ^ bit) for i in range(peers)])  53.9 us
    ppermute x21, starting transfers between devices, exchange(): return lax.ppermute(x, axis, [(i, i ^ bit) for i in range(peers)])  26 us
    pallas_call x1, Pallas kernels, contract_near(): pl.pallas_call(body, out_shape=[jax.ShapeDtypeStruct((lam, cols), F32), j...  6.4 us
    pallas_call x2, Pallas kernels, pack_integrals(): pl.pallas_call(body, out_shape=out_shape, in_specs=[SMEM_SPEC, SMEM_SPEC,...  5.23 us
    pallas_call x1, Pallas kernels, pack_density(): pl.pallas_call(body, out_shape=[jax.ShapeDtypeStruct((n, sum_size), BF16)...  4.05 us
    pallas_call x1, Pallas kernels, contract_last(): pl.pallas_call(body, out_shape=jax.ShapeDtypeStruct((rows, wide), BF16),...  3.42 us
    pallas_call x2, Pallas kernels, pack_part(): pl.pallas_call(body, out_shape=jax.ShapeDtypeStruct((size, cols), BF16),...  2.41 us
  transfers between devices with their start and end apart: 21, of which 8 were waited for; matrix products, arithmetic and copies ran while one was open for 0% of the time, Pallas kernels for 16%

profile of v1, /device:TPU:0, one launch (start us, length us, event | category | flops | bytes accessed | tf_op | source)
XLA Modules:
  0.0 107.7 jit_solution(5293021494853141683)
XLA Ops:
  0.0 1.3 %first_fit.1 = s32[1]{0:T(128)} custom-call(s32[128]{0:T(128)} %count_ref.1, s32[48]{0:T(128)} %ri_ref.1), custom_call_target="tpu_custom_call" | custom-call | tf_op jit(solution)/shard_map/first_fit/pallas_call | solution.py:99
  2.0 104.6 %conditional.3 = (bf16[1024,768]{1,0:T(8,128)(2,1)S(1)}) conditional(s32[]{:T(128)} %convert_element_type.9, (s32[]{:T(128)}, s32[128]{0:T(128)}, s32[32,16]{0,1:T(8,128)}, bf16[1024,512]{1,0:T(8,128)(2,1)}, s32[48]{0:T(128)}, /*index=5*/s32[4,48]{1,0:T(4,128)}, bf16[128,6144]{1,0:T(8,128)(2,1)}) %tuple.62, (s32[128]{0:T(128)}, s32[32,16]{0,1:T(8,128)}, ...), branch_computations={%region_0.0_spmd, %region_5.0_spmd} | conditional | flops 14092861440 | bytes 89402256 | solution.py:488
  2.2 3.0 %pack_other_core.7 = bf16[4,128,640]{2,1,0:T(8,128)(2,1)S(1)} custom-call(s32[128]{0:T(128)} %get-tuple-element.189.count_ref, s32[48]{0:T(128)} %get-tuple-element.193.ri_ref, s32[4,48]{1,0:T(4,128)} %get-tuple-element.194.mask_ref, bf16[128,6144]{1,0:T(8,128)(2,1)} %get-tuple-element.195.x_ref), custom_call_target="tpu_custom_call" | custom-call | flops 503316480 | bytes 1769472 | tf_op jit(solution)/shard_map/cond/branch_1_fun/pack_other_core/pallas_call | solution.py:149
  5.9 4.0 %pack_density.7 = (bf16[768,384]{1,0:T(8,128)(2,1)S(1)}, bf16[256,384]{1,0:T(8,128)(2,1)S(1)}, bf16[512,384]{1,0:T(8,128)(2,1)S(1)}) custom-call(s32[128]{0:T(128)S(1)} %copy-done.12, s32[32,16]{1,0:T(8,128)S(1)} %copy.10.mask_ref, bf16[1024,512]{1,0:T(8,128)(2,1)} %get-tuple-element.191.x_ref), custom_call_target="tpu_custom_call" | custom-call | flops 1006632960 | bytes 1048576 | tf_op jit(solution)/shard_map/cond/branch_1_fun/pack_density/pallas_call | solution.py:198
  10.2 2.2 %pack_own_core.7 = (bf16[256,640]{1,0:T(8,128)(2,1)S(1)}, bf16[256,640]{1,0:T(8,128)(2,1)S(1)}, bf16[256,640]{1,0:T(8,128)(2,1)S(1)}, bf16[256,640]{1,0:T(8,128)(2,1)S(1)}) custom-call(s32[128]{0:T(128)S(1)} %copy-done.12, s32[48]{0:T(128)S(1)} %copy-done.16, s32[4,48]{1,0:T(4,128)S(1)} %copy-done.8, bf16[128,6144]{1,0:T(8,128)(2,1)S(1)} %copy-done.3, ...), custom_call_target="tpu_custom_call" | custom-call | flops 503316480 | bytes 1769472 | tf_op jit(solution)/shard_map/cond/branch_1_fun/pack_own_core/pallas_call | solution.py:149
  12.4 3.0 %collective-permute-start.68 = (bf16[256,640]{1,0:T(8,128)(2,1)S(1)}, bf16[256,640]{1,0:T(8,128)(2,1)S(1)}, u32[]{:S(2)}, u32[]{:S(2)}) collective-permute-start(bf16[256,640]{1,0:T(8,128)(2,1)S(1)} %get-tuple-element.204), channel_id=1, source_target_pairs={{0,2},{1,3},{2,0},{3,1},{4,6},{5,7},{6,4},{7,5},{8,10},{9,11},{10,... | collective-permute-start | bytes 983048 | tf_op jit(solution)/shard_map/cond/branch_1_fun/ppermute | solution.py:244
  15.4 2.6 %collective-permute-start.67 = (bf16[256,384]{1,0:T(8,128)(2,1)S(1)}, bf16[256,384]{1,0:T(8,128)(2,1)S(1)}, u32[]{:S(2)}, u32[]{:S(2)}) collective-permute-start(bf16[256,384]{1,0:T(8,128)(2,1)S(1)} %get-tuple-element.202), channel_id=1, source_target_pairs={{0,4},{1,5},{2,6},{3,7},{4,0},{5,1},{6,2},{7,3},{8,12},{9,13},{10,... | collective-permute-start | bytes 589832 | tf_op jit(solution)/shard_map/cond/branch_1_fun/ppermute | solution.py:244
  18.3 2.5 %collective-permute-start.65 = (bf16[256,640]{1,0:T(8,128)(2,1)S(1)}, bf16[256,640]{1,0:T(8,128)(2,1)S(1)}, u32[]{:S(2)}, u32[]{:S(2)}) collective-permute-start(bf16[256,640]{1,0:T(8,128)(2,1)S(1)} %get-tuple-element.200), channel_id=1, source_target_pairs={{0,6},{1,7},{2,4},{3,5},{4,2},{5,3},{6,0},{7,1},{8,14},{9,15},{10,... | collective-permute-start | bytes 983048 | tf_op jit(solution)/shard_map/cond/branch_1_fun/ppermute | solution.py:244
  20.8 6.9 %collective-permute-done.67.refs_0_ = bf16[256,384]{1,0:T(8,128)(2,1)S(1)} collective-permute-done((bf16[256,384]{1,0:T(8,128)(2,1)S(1)}, bf16[256,384]{1,0:T(8,128)(2,1)S(1)}, u32[]{:S(2)}, u32[]{:S(2)}) %collective-permute-start.67) | collective-permute-done | bytes 196640 | tf_op jit(solution)/shard_map/cond/branch_1_fun/ppermute | solution.py:244
  27.8 2.6 %collective-permute-done.68.refs_1_ = bf16[256,640]{1,0:T(8,128)(2,1)S(1)} collective-permute-done((bf16[256,640]{1,0:T(8,128)(2,1)S(1)}, bf16[256,640]{1,0:T(8,128)(2,1)S(1)}, u32[]{:S(2)}, u32[]{:S(2)}) %collective-permute-start.68) | collective-permute-done | bytes 327712 | tf_op jit(solution)/shard_map/cond/branch_1_fun/ppermute | solution.py:244
  31.5 1.7 %collective-permute-start.69 = (bf16[384,640]{1,0:T(8,128)(2,1)S(1)}, bf16[384,640]{1,0:T(8,128)(2,1)S(1)}, u32[]{:S(2)}, u32[]{:S(2)}) collective-permute-start(bf16[384,640]{1,0:T(8,128)(2,1)S(1)} %pack_part.15.refs_4_), channel_id=1, source_target_pairs={{0,8},{8,0},{16,24},{24,16},{1,9},{9,1},{17,25},{25,17},{2,10},{10... | collective-permute-start | bytes 1474568 | tf_op jit(solution)/shard_map/cond/branch_1_fun/ppermute | solution.py:244
  33.2 1.5 %collective-permute-start.70 = (bf16[384,640]{1,0:T(8,128)(2,1)S(1)}, bf16[384,640]{1,0:T(8,128)(2,1)S(1)}, u32[]{:S(2)}, u32[]{:S(2)}) collective-permute-start(bf16[384,640]{1,0:T(8,128)(2,1)S(1)} %pack_part.15.refs_4_), channel_id=1, source_target_pairs={{0,16},{8,24},{16,0},{24,8},{1,17},{9,25},{17,1},{25,9},{2,18},{10... | collective-permute-start | bytes 1474568 | tf_op jit(solution)/shard_map/cond/branch_1_fun/ppermute | solution.py:244
  36.7 12.7 %collective-permute-done.64.refs_0_ = bf16[256,640]{1,0:T(8,128)(2,1)S(1)} collective-permute-done((bf16[256,640]{1,0:T(8,128)(2,1)S(1)}, bf16[256,640]{1,0:T(8,128)(2,1)S(1)}, u32[]{:S(2)}, u32[]{:S(2)}) %collective-permute-start.64) | collective-permute-done | bytes 327712 | tf_op jit(solution)/shard_map/cond/branch_1_fun/ppermute | solution.py:244
  50.6 1.6 %collective-permute-done.71.refs_0_ = bf16[256,384]{1,0:T(8,128)(2,1)S(1)} collective-permute-done((bf16[256,384]{1,0:T(8,128)(2,1)S(1)}, bf16[256,384]{1,0:T(8,128)(2,1)S(1)}, u32[]{:S(2)}, u32[]{:S(2)}) %collective-permute-start.71) | collective-permute-done | bytes 196640 | tf_op jit(solution)/shard_map/cond/branch_1_fun/ppermute | solution.py:244
  52.2 5.0 %collective-permute-start.72 = (bf16[768,384]{1,0:T(8,128)(2,1)S(1)}, bf16[768,384]{1,0:T(8,128)(2,1)S(1)}, u32[]{:S(2)}, u32[]{:S(2)}) collective-permute-start(bf16[768,384]{1,0:T(8,128)(2,1)S(1)} %get-tuple-element.207.refs_0_), channel_id=1, source_target_pairs={{0,2},{1,3},{2,0},{3,1},{4,6},{5,7},{6,4},{7,5},{8,10},{9,11},{10,... | collective-permute-start | bytes 1769480 | tf_op jit(solution)/shard_map/cond/branch_1_fun/ppermute | solution.py:244
  57.2 1.5 %collective-permute-start.75 = (bf16[384,640]{1,0:T(8,128)(2,1)S(1)}, bf16[384,640]{1,0:T(8,128)(2,1)S(1)}, u32[]{:S(2)}, u32[]{:S(2)}) collective-permute-start(bf16[384,640]{1,0:T(8,128)(2,1)S(1)} %pack_part.14.refs_5_), channel_id=1, source_target_pairs={{0,16},{8,24},{16,0},{24,8},{1,17},{9,25},{17,1},{25,9},{2,18},{10... | collective-permute-start | bytes 1474568 | tf_op jit(solution)/shard_map/cond/branch_1_fun/ppermute | solution.py:244
  58.7 1.5 %collective-permute-start.74 = (bf16[384,640]{1,0:T(8,128)(2,1)S(1)}, bf16[384,640]{1,0:T(8,128)(2,1)S(1)}, u32[]{:S(2)}, u32[]{:S(2)}) collective-permute-start(bf16[384,640]{1,0:T(8,128)(2,1)S(1)} %pack_part.14.refs_5_), channel_id=1, source_target_pairs={{0,8},{8,0},{16,24},{24,16},{1,9},{9,1},{17,25},{25,17},{2,10},{10... | collective-permute-start | bytes 1474568 | tf_op jit(solution)/shard_map/cond/branch_1_fun/ppermute | solution.py:244
  61.3 16.8 %collective-permute-done.72.refs_2_ = bf16[768,384]{1,0:T(8,128)(2,1)S(1)} collective-permute-done((bf16[768,384]{1,0:T(8,128)(2,1)S(1)}, bf16[768,384]{1,0:T(8,128)(2,1)S(1)}, u32[]{:S(2)}, u32[]{:S(2)}) %collective-permute-start.72) | collective-permute-done | bytes 589856 | tf_op jit(solution)/shard_map/cond/branch_1_fun/ppermute | solution.py:244
  78.2 1.5 %collective-permute-start.76 = (bf16[384,640]{1,0:T(8,128)(2,1)S(1)}, bf16[384,640]{1,0:T(8,128)(2,1)S(1)}, u32[]{:S(2)}, u32[]{:S(2)}) collective-permute-start(bf16[384,640]{1,0:T(8,128)(2,1)S(1)} %collective-permute-done.69.refs_6_), channel_id=1, source_target_pairs={{0,16},{8,24},{16,0},{24,8},{1,17},{9,25},{17,1},{25,9},{2,18},{10... | collective-permute-start | bytes 1474568 | tf_op jit(solution)/shard_map/cond/branch_1_fun/ppermute | solution.py:244
  79.7 1.5 %collective-permute-start.77 = (bf16[384,640]{1,0:T(8,128)(2,1)S(1)}, bf16[384,640]{1,0:T(8,128)(2,1)S(1)}, u32[]{:S(2)}, u32[]{:S(2)}) collective-permute-start(bf16[384,640]{1,0:T(8,128)(2,1)S(1)} %collective-permute-done.75.refs_9_), channel_id=1, source_target_pairs={{0,8},{8,0},{16,24},{24,16},{1,9},{9,1},{17,25},{25,17},{2,10},{10... | collective-permute-start | bytes 1474568 | tf_op jit(solution)/shard_map/cond/branch_1_fun/ppermute | solution.py:244
  81.3 10.5 %collective-permute-done.76.refs_10_ = bf16[384,640]{1,0:T(8,128)(2,1)S(1)} collective-permute-done((bf16[384,640]{1,0:T(8,128)(2,1)S(1)}, bf16[384,640]{1,0:T(8,128)(2,1)S(1)}, u32[]{:S(2)}, u32[]{:S(2)}) %collective-permute-start.76) | collective-permute-done | bytes 491552 | tf_op jit(solution)/shard_map/cond/branch_1_fun/ppermute | solution.py:244
  93.0 6.4 %contract_near.7 = (f32[768,640]{1,0:T(8,128)S(1)}, bf16[4,384,640]{2,1,0:T(8,128)(2,1)S(1)}) custom-call(bf16[768,384]{1,0:T(8,128)(2,1)S(1)} %get-tuple-element.207.refs_0_, bf16[768,384]{1,0:T(8,128)(2,1)S(1)} %collective-permute-done.66.refs_1_, bf16[768,384]{1,0:T(8,128)(2,1)S(1)} %collective-permute-done.72.refs_2_, ...), custom_call_target="tpu_custom_call" | custom-call | flops 1509949440 | bytes 4325376 | tf_op jit(solution)/shard_map/cond/branch_1_fun/contract_near/pallas_call | solution.py:344
  101.4 1.5 %collective-permute-done.82.refs_2_ = bf16[256,384]{1,0:T(8,128)(2,1)S(1)} collective-permute-done((bf16[256,384]{1,0:T(8,128)(2,1)S(1)}, bf16[256,384]{1,0:T(8,128)(2,1)S(1)}, u32[]{:S(2)}, u32[]{:S(2)}) %collective-permute-start.82) | collective-permute-done | bytes 196640 | tf_op jit(solution)/shard_map/cond/branch_1_fun/ppermute | solution.py:244
  102.9 3.4 %contract_last.7 = bf16[1024,768]{1,0:T(8,128)(2,1)S(1)} custom-call(f32[768,640]{1,0:T(8,128)S(1)} %contract_far.7.before, bf16[4,384,640]{2,1,0:T(8,128)(2,1)S(1)} %get-tuple-element.210.s_ref, bf16[1024,768]{1,0:T(8,128)(2,1)S(1)} %get-tuple-element.198.lam_hot, bf16[640,768]{1,0:T(8,128)(2,1)S(1)} %get-tuple-element.213.col_hot, ...), custom_call_target="tpu_custom_call" | custom-call | flops 754974720 | bytes 2162688 | tf_op jit(solution)/shard_map/cond/branch_1_fun/contract_last/pallas_call | solution.py:404
  (42 shorter events, 11.0 us)
Async XLA Ops:
  5.3 4.9 %copy-start.3 = (bf16[128,6144]{1,0:T(8,128)(2,1)S(1)}, bf16[128,6144]{1,0:T(8,128)(2,1)}, u32[]{:S(2)}) copy-start(bf16[128,6144]{1,0:T(8,128)(2,1)} %get-tuple-element.195.x_ref) | copy-start | bytes 4718596 | tf_op jit(solution)/shard_map/cond
  5.3 4.9 %copy-start.8 = (s32[4,48]{1,0:T(4,128)S(1)}, s32[4,48]{1,0:T(4,128)}, u32[]{:S(2)}) copy-start(s32[4,48]{1,0:T(4,128)} %get-tuple-element.194.mask_ref) | copy-start | bytes 2308 | tf_op jit(solution)/shard_map/cond
  5.3 4.9 %copy-start.16 = (s32[48]{0:T(128)S(1)}, s32[48]{0:T(128)}, u32[]{:S(2)}) copy-start(s32[48]{0:T(128)} %get-tuple-element.193.ri_ref) | copy-start | bytes 580 | tf_op jit(solution)/shard_map/cond
  5.3 4.9 %collective-permute-start.63 = (bf16[4,128,640]{2,1,0:T(8,128)(2,1)S(1)}, bf16[4,128,640]{2,1,0:T(8,128)(2,1)S(1)}, u32[]{:S(2)}, u32[]{:S(2)}) collective-permute-start(bf16[4,128,640]{2,1,0:T(8,128)(2,1)S(1)} %pack_other_core.7), channel_id=1, source_target_pairs={{0,1},{1,0},{2,3},{3,2},{4,5},{5,4},{6,7},{7,6},{8,9},{9,8},{10,11... | collective-permute-start | bytes 1966088 | tf_op jit(solution)/shard_map/cond/branch_1_fun/ppermute | solution.py:244
  9.9 17.8 %collective-permute-start.66 = (bf16[768,384]{1,0:T(8,128)(2,1)S(1)}, bf16[768,384]{1,0:T(8,128)(2,1)S(1)}, u32[]{:S(2)}, u32[]{:S(2)}) collective-permute-start(bf16[768,384]{1,0:T(8,128)(2,1)S(1)} %get-tuple-element.207.refs_0_), channel_id=1, source_target_pairs={{0,1},{1,0},{2,3},{3,2},{4,5},{5,4},{6,7},{7,6},{8,9},{9,8},{10,11... | collective-permute-start | bytes 1769480 | tf_op jit(solution)/shard_map/cond/branch_1_fun/ppermute | solution.py:244
  12.4 17.9 %collective-permute-start.68 = (bf16[256,640]{1,0:T(8,128)(2,1)S(1)}, bf16[256,640]{1,0:T(8,128)(2,1)S(1)}, u32[]{:S(2)}, u32[]{:S(2)}) collective-permute-start(bf16[256,640]{1,0:T(8,128)(2,1)S(1)} %get-tuple-element.204), channel_id=1, source_target_pairs={{0,2},{1,3},{2,0},{3,1},{4,6},{5,7},{6,4},{7,5},{8,10},{9,11},{10,... | collective-permute-start | bytes 983048 | tf_op jit(solution)/shard_map/cond/branch_1_fun/ppermute | solution.py:244
  15.4 12.3 %collective-permute-start.67 = (bf16[256,384]{1,0:T(8,128)(2,1)S(1)}, bf16[256,384]{1,0:T(8,128)(2,1)S(1)}, u32[]{:S(2)}, u32[]{:S(2)}) collective-permute-start(bf16[256,384]{1,0:T(8,128)(2,1)S(1)} %get-tuple-element.202), channel_id=1, source_target_pairs={{0,4},{1,5},{2,6},{3,7},{4,0},{5,1},{6,2},{7,3},{8,12},{9,13},{10,... | collective-permute-start | bytes 589832 | tf_op jit(solution)/shard_map/cond/branch_1_fun/ppermute | solution.py:244
  18.0 31.4 %collective-permute-start.64 = (bf16[256,640]{1,0:T(8,128)(2,1)S(1)}, bf16[256,640]{1,0:T(8,128)(2,1)S(1)}, u32[]{:S(2)}, u32[]{:S(2)}) collective-permute-start(bf16[256,640]{1,0:T(8,128)(2,1)S(1)} %get-tuple-element.197), channel_id=1, source_target_pairs={{0,4},{1,5},{2,6},{3,7},{4,0},{5,1},{6,2},{7,3},{8,12},{9,13},{10,... | collective-permute-start | bytes 983048 | tf_op jit(solution)/shard_map/cond/branch_1_fun/ppermute | solution.py:244
  18.3 31.1 %collective-permute-start.65 = (bf16[256,640]{1,0:T(8,128)(2,1)S(1)}, bf16[256,640]{1,0:T(8,128)(2,1)S(1)}, u32[]{:S(2)}, u32[]{:S(2)}) collective-permute-start(bf16[256,640]{1,0:T(8,128)(2,1)S(1)} %get-tuple-element.200), channel_id=1, source_target_pairs={{0,6},{1,7},{2,4},{3,5},{4,2},{5,3},{6,0},{7,1},{8,14},{9,15},{10,... | collective-permute-start | bytes 983048 | tf_op jit(solution)/shard_map/cond/branch_1_fun/ppermute | solution.py:244
  31.5 20.7 %collective-permute-start.69 = (bf16[384,640]{1,0:T(8,128)(2,1)S(1)}, bf16[384,640]{1,0:T(8,128)(2,1)S(1)}, u32[]{:S(2)}, u32[]{:S(2)}) collective-permute-start(bf16[384,640]{1,0:T(8,128)(2,1)S(1)} %pack_part.15.refs_4_), channel_id=1, source_target_pairs={{0,8},{8,0},{16,24},{24,16},{1,9},{9,1},{17,25},{25,17},{2,10},{10... | collective-permute-start | bytes 1474568 | tf_op jit(solution)/shard_map/cond/branch_1_fun/ppermute | solution.py:244
  33.2 19.0 %collective-permute-start.70 = (bf16[384,640]{1,0:T(8,128)(2,1)S(1)}, bf16[384,640]{1,0:T(8,128)(2,1)S(1)}, u32[]{:S(2)}, u32[]{:S(2)}) collective-permute-start(bf16[384,640]{1,0:T(8,128)(2,1)S(1)} %pack_part.15.refs_4_), channel_id=1, source_target_pairs={{0,16},{8,24},{16,0},{24,8},{1,17},{9,25},{17,1},{25,9},{2,18},{10... | collective-permute-start | bytes 1474568 | tf_op jit(solution)/shard_map/cond/branch_1_fun/ppermute | solution.py:244
  35.8 16.4 %collective-permute-start.71 = (bf16[256,384]{1,0:T(8,128)(2,1)S(1)}, bf16[256,384]{1,0:T(8,128)(2,1)S(1)}, u32[]{:S(2)}, u32[]{:S(2)}) collective-permute-start(bf16[256,384]{1,0:T(8,128)(2,1)S(1)} %collective-permute-done.67.refs_0_), channel_id=1, source_target_pairs={{0,2},{1,3},{2,0},{3,1},{4,6},{5,7},{6,4},{7,5},{8,10},{9,11},{10,... | collective-permute-start | bytes 589832 | tf_op jit(solution)/shard_map/cond/branch_1_fun/ppermute | solution.py:244
  52.2 25.9 %collective-permute-start.72 = (bf16[768,384]{1,0:T(8,128)(2,1)S(1)}, bf16[768,384]{1,0:T(8,128)(2,1)S(1)}, u32[]{:S(2)}, u32[]{:S(2)}) collective-permute-start(bf16[768,384]{1,0:T(8,128)(2,1)S(1)} %get-tuple-element.207.refs_0_), channel_id=1, source_target_pairs={{0,2},{1,3},{2,0},{3,1},{4,6},{5,7},{6,4},{7,5},{8,10},{9,11},{10,... | collective-permute-start | bytes 1769480 | tf_op jit(solution)/shard_map/cond/branch_1_fun/ppermute | solution.py:244
  57.2 20.9 %collective-permute-start.75 = (bf16[384,640]{1,0:T(8,128)(2,1)S(1)}, bf16[384,640]{1,0:T(8,128)(2,1)S(1)}, u32[]{:S(2)}, u32[]{:S(2)}) collective-permute-start(bf16[384,640]{1,0:T(8,128)(2,1)S(1)} %pack_part.14.refs_5_), channel_id=1, source_target_pairs={{0,16},{8,24},{16,0},{24,8},{1,17},{9,25},{17,1},{25,9},{2,18},{10... | collective-permute-start | bytes 1474568 | tf_op jit(solution)/shard_map/cond/branch_1_fun/ppermute | solution.py:244
  58.7 22.4 %collective-permute-start.74 = (bf16[384,640]{1,0:T(8,128)(2,1)S(1)}, bf16[384,640]{1,0:T(8,128)(2,1)S(1)}, u32[]{:S(2)}, u32[]{:S(2)}) collective-permute-start(bf16[384,640]{1,0:T(8,128)(2,1)S(1)} %pack_part.14.refs_5_), channel_id=1, source_target_pairs={{0,8},{8,0},{16,24},{24,16},{1,9},{9,1},{17,25},{25,17},{2,10},{10... | collective-permute-start | bytes 1474568 | tf_op jit(solution)/shard_map/cond/branch_1_fun/ppermute | solution.py:244
  60.2 20.9 %collective-permute-start.78 = (bf16[512,384]{1,0:T(8,128)(2,1)S(1)}, bf16[512,384]{1,0:T(8,128)(2,1)S(1)}, u32[]{:S(2)}, u32[]{:S(2)}) collective-permute-start(bf16[512,384]{1,0:T(8,128)(2,1)S(1)} %get-tuple-element.212), channel_id=1, source_target_pairs={{0,4},{1,5},{2,6},{3,7},{4,0},{5,1},{6,2},{7,3},{8,12},{9,13},{10,... | collective-permute-start | bytes 1179656 | tf_op jit(solution)/shard_map/cond/branch_1_fun/ppermute | solution.py:244
  78.2 14.9 %collective-permute-start.73 = (bf16[768,384]{1,0:T(8,128)(2,1)S(1)}, bf16[768,384]{1,0:T(8,128)(2,1)S(1)}, u32[]{:S(2)}, u32[]{:S(2)}) collective-permute-start(bf16[768,384]{1,0:T(8,128)(2,1)S(1)} %collective-permute-done.72.refs_2_), channel_id=1, source_target_pairs={{0,1},{1,0},{2,3},{3,2},{4,5},{5,4},{6,7},{7,6},{8,9},{9,8},{10,11... | collective-permute-start | bytes 1769480 | tf_op jit(solution)/shard_map/cond/branch_1_fun/ppermute | solution.py:244
  78.2 13.6 %collective-permute-start.76 = (bf16[384,640]{1,0:T(8,128)(2,1)S(1)}, bf16[384,640]{1,0:T(8,128)(2,1)S(1)}, u32[]{:S(2)}, u32[]{:S(2)}) collective-permute-start(bf16[384,640]{1,0:T(8,128)(2,1)S(1)} %collective-permute-done.69.refs_6_), channel_id=1, source_target_pairs={{0,16},{8,24},{16,0},{24,8},{1,17},{9,25},{17,1},{25,9},{2,18},{10... | collective-permute-start | bytes 1474568 | tf_op jit(solution)/shard_map/cond/branch_1_fun/ppermute | solution.py:244
  79.7 13.4 %collective-permute-start.77 = (bf16[384,640]{1,0:T(8,128)(2,1)S(1)}, bf16[384,640]{1,0:T(8,128)(2,1)S(1)}, u32[]{:S(2)}, u32[]{:S(2)}) collective-permute-start(bf16[384,640]{1,0:T(8,128)(2,1)S(1)} %collective-permute-done.75.refs_9_), channel_id=1, source_target_pairs={{0,8},{8,0},{16,24},{24,16},{1,9},{9,1},{17,25},{25,17},{2,10},{10... | collective-permute-start | bytes 1474568 | tf_op jit(solution)/shard_map/cond/branch_1_fun/ppermute | solution.py:244
  81.2 18.3 %collective-permute-start.80 = (bf16[512,384]{1,0:T(8,128)(2,1)S(1)}, bf16[512,384]{1,0:T(8,128)(2,1)S(1)}, u32[]{:S(2)}, u32[]{:S(2)}) collective-permute-start(bf16[512,384]{1,0:T(8,128)(2,1)S(1)} %collective-permute-done.78.refs_1_), channel_id=1, source_target_pairs={{0,1},{1,0},{2,3},{3,2},{4,5},{5,4},{6,7},{7,6},{8,9},{9,8},{10,11... | collective-permute-start | bytes 1179656 | tf_op jit(solution)/shard_map/cond/branch_1_fun/ppermute | solution.py:244
  81.2 19.6 %collective-permute-start.81 = (bf16[512,384]{1,0:T(8,128)(2,1)S(1)}, bf16[512,384]{1,0:T(8,128)(2,1)S(1)}, u32[]{:S(2)}, u32[]{:S(2)}) collective-permute-start(bf16[512,384]{1,0:T(8,128)(2,1)S(1)} %collective-permute-done.78.refs_1_), channel_id=1, source_target_pairs={{0,2},{1,3},{2,0},{3,1},{4,6},{5,7},{6,4},{7,5},{8,10},{9,11},{10,... | collective-permute-start | bytes 1179656 | tf_op jit(solution)/shard_map/cond/branch_1_fun/ppermute | solution.py:244
  91.8 7.7 %collective-permute-start.79 = (bf16[256,384]{1,0:T(8,128)(2,1)S(1)}, bf16[256,384]{1,0:T(8,128)(2,1)S(1)}, u32[]{:S(2)}, u32[]{:S(2)}) collective-permute-start(bf16[256,384]{1,0:T(8,128)(2,1)S(1)} %collective-permute-done.67.refs_0_), channel_id=1, source_target_pairs={{0,1},{1,0},{2,3},{3,2},{4,5},{5,4},{6,7},{7,6},{8,9},{9,8},{10,11... | collective-permute-start | bytes 589832 | tf_op jit(solution)/shard_map/cond/branch_1_fun/ppermute | solution.py:244
  100.8 2.1 %collective-permute-start.83 = (bf16[512,384]{1,0:T(8,128)(2,1)S(1)}, bf16[512,384]{1,0:T(8,128)(2,1)S(1)}, u32[]{:S(2)}, u32[]{:S(2)}) collective-permute-start(bf16[512,384]{1,0:T(8,128)(2,1)S(1)} %collective-permute-done.81.refs_1_), channel_id=1, source_target_pairs={{0,1},{1,0},{2,3},{3,2},{4,5},{5,4},{6,7},{7,6},{8,9},{9,8},{10,11... | collective-permute-start | bytes 1179656 | tf_op jit(solution)/shard_map/cond/branch_1_fun/ppermute | solution.py:244
  100.9 2.0 %collective-permute-start.82 = (bf16[256,384]{1,0:T(8,128)(2,1)S(1)}, bf16[256,384]{1,0:T(8,128)(2,1)S(1)}, u32[]{:S(2)}, u32[]{:S(2)}) collective-permute-start(bf16[256,384]{1,0:T(8,128)(2,1)S(1)} %collective-permute-done.71.refs_0_), channel_id=1, source_target_pairs={{0,1},{1,0},{2,3},{3,2},{4,5},{5,4},{6,7},{7,6},{8,9},{9,8},{10,11... | collective-permute-start | bytes 589832 | tf_op jit(solution)/shard_map/cond/branch_1_fun/ppermute | solution.py:244
  (3 other events, 8.4 us)
